TPU v7x, 1024 devices: a whole 8x8x8 slice. The times are simulated.
1024 devices in a mesh: lat: 64 (over x, z), agg: 16 (over y, core).
Axes of the slice: x: 8, y: 8, z: 8, core: 2. Of those that a mesh axis runs over, the one named last changes fastest.
Arguments:
- solution: float32 [12, 256, 64, 128], P(None, 'lat', 'agg'), may hold values from -6 to 6
- right_side: float32 [12, 256, 64, 128], P(None, 'lat', 'agg'), may hold values from -6 to 6
- links: bfloat16 [4, 3, 3, 256, 64, 128], P(None, None, None, 'lat', 'agg'), may hold values from -3.5 to 3.5
- clover: bfloat16 [2, 6, 6, 256, 64, 128], P(None, None, None, 'lat', 'agg'), may hold values from -2.5 to 2.5
- null_vectors: bfloat16 [48, 12, 256, 64, 128], P(None, None, 'lat', 'agg'), may hold values from -0.109375 to 0.109375
- coarse_inverse: bfloat16 [64, 16, 8, 48, 48], P('lat', 'agg'), may hold values from -0.875 to 0.875
- coarse_links: bfloat16 [8, 64, 16, 8, 48, 48], P(None, 'lat', 'agg'), may hold values from -0.15625 to 0.15625
Outputs:
- updated: float32 [12, 256, 64, 128], P(None, 'lat', 'agg')
- residual_after: float32 [12, 256, 64, 128], P(None, 'lat', 'agg')
All inputs are finite; a program needn't handle non-finite values.
Results may differ from a plain program's by a relative error of at most 0.0075.
Values sent between devices are 32-bit elements; how exact they have to be, the bound alone decides.
No kernel may reach another device: no remote copies, remote signals or barrier semaphores. Data moves between devices by JAX's collectives and lax.ppermute only.
A program may use at most 32 MiB of HBM per device.

v0:
```python
import jax
import jax.numpy as jnp
import numpy as np
from jax import lax
from jax.sharding import PartitionSpec as P

CY = 8
CZ = 16
SWEEPS = 2


exact_mode = lax.Precision.HIGHEST
hopping = 0.5
wilson_mass = 4.0


def padded_2(value, sides, width):
    for axis, dim in sides:
        size, length = (lax.axis_size(axis), value.shape[dim])
        up = [(i, (i + 1) % size) for i in range(size)]
        down = [(j, i) for i, j in up]
        last = lax.slice_in_dim(value, length - width, length, axis=dim)
        leading = lax.slice_in_dim(value, 0, width, axis=dim)
        before = lax.ppermute(last, axis, up)
        after = lax.ppermute(leading, axis, down)
        value = jnp.concatenate([before, value, after], axis=dim)
    return value


def gamma_table():
    table = np.zeros((4, 4, 4), np.float32)
    table[0] = [[0, 0, 1, 0], [0, 0, 0, 1], [1, 0, 0, 0], [0, 1, 0, 0]]
    table[1] = [[0, 0, 0, 1], [0, 0, 1, 0], [0, 1, 0, 0], [1, 0, 0, 0]]
    table[2] = [[1, 0, 0, 0], [0, 1, 0, 0], [0, 0, -1, 0], [0, 0, 0, -1]]
    table[3] = [[0, 1, 0, 0], [1, 0, 0, 0], [0, 0, 0, -1], [0, 0, -1, 0]]
    return table


def spin_apply(matrix, spinor):
    return jnp.einsum(
        "st,t...->s...", jnp.asarray(matrix, spinor.dtype), spinor, precision=exact_mode
    )


def color_apply(transport, spinor):
    total = transport[None, :, 0] * spinor[:, None, 0]
    for inner in range(1, 3):
        total = total + transport[None, :, inner] * spinor[:, None, inner]
    return total


def plane_step(values, axis, direction):
    plane = values.shape[-1]
    if axis == 2:
        return jnp.roll(values, -direction * CZ, axis=-1)
    places = jnp.arange(plane, dtype=jnp.int32) % CZ
    if direction == 1:
        inside = jnp.roll(values, -1, axis=-1)
        wrapped = jnp.roll(values, CZ - 1, axis=-1)
        return jnp.where(places == CZ - 1, wrapped, inside)
    inside = jnp.roll(values, 1, axis=-1)
    wrapped = jnp.roll(values, -(CZ - 1), axis=-1)
    return jnp.where(places == 0, wrapped, inside)


def block_matrix(plane):
    places = jnp.arange(plane, dtype=jnp.int32)
    owners = places // CZ // 4 * (CZ // 4) + places % CZ // 4
    targets = jnp.arange(CY // 4 * (CZ // 4), dtype=jnp.int32)
    return owners[:, None] == targets[None, :]


def dirac(field, links, clover):
    depth, width, plane = (field.shape[1], field.shape[2], field.shape[3])
    flat4 = (4, 3, depth, width, plane)
    spinor = field.reshape(flat4)
    transport = links.astype(jnp.float32)
    halves = field.reshape((2, 6, depth, width, plane))
    blocks = clover.astype(jnp.float32)
    local = blocks[:, :, 0] * halves[:, None, 0]
    for inner in range(1, 6):
        local = local + blocks[:, :, inner] * halves[:, None, inner]
    gammas = gamma_table()
    identity = np.eye(4, dtype=np.float32)
    moved_time = color_apply(jnp.swapaxes(transport[0], 0, 1), spinor)
    moved_space = color_apply(jnp.swapaxes(transport[1], 0, 1), spinor)
    stacked = jnp.concatenate([spinor, moved_time, moved_space], axis=0).reshape(
        36, depth, width, plane
    )
    padded = padded_2(stacked, (("lat", 1), ("agg", 2)), 1)
    ahead_time = spin_apply(identity - gammas[0], padded[0:12, 2:, 1:-1].reshape(flat4))
    back_time = spin_apply(identity + gammas[0], padded[12:24, :-2, 1:-1].reshape(flat4))
    ahead_space = spin_apply(identity - gammas[1], padded[0:12, 1:-1, 2:].reshape(flat4))
    back_space = spin_apply(identity + gammas[1], padded[24:36, 1:-1, :-2].reshape(flat4))
    hops = color_apply(transport[0], ahead_time) + back_time
    hops = hops + color_apply(transport[1], ahead_space) + back_space
    for axis in (2, 3):
        ahead = plane_step(spinor, axis, 1)
        forward = color_apply(transport[axis], spin_apply(identity - gammas[axis], ahead))
        moved = color_apply(jnp.swapaxes(transport[axis], 0, 1), spinor)
        backward = spin_apply(identity + gammas[axis], plane_step(moved, axis, -1))
        hops = hops + forward + backward
    total = wilson_mass * spinor + local.reshape(flat4) - hopping * hops
    return total.reshape(field.shape)


def restrict(rough, null_vectors):
    channels, depth, width, plane = (
        null_vectors.shape[0],
        rough.shape[1],
        rough.shape[2],
        rough.shape[3],
    )
    summed = jnp.einsum("kmtxp,mtxp->ktxp", null_vectors, rough, preferred_element_type=jnp.float32)
    summed = summed.reshape(channels, depth // 4, 4, width // 4, 4, plane).sum(axis=(2, 4))
    selector = block_matrix(plane).astype(jnp.float32)
    coarse = jnp.einsum("ktxp,pc->ktxc", summed, selector, precision=exact_mode)
    return jnp.transpose(coarse, (1, 2, 3, 0))


def prolong(coarse_rounded, null_vectors):
    channels, depth, width, plane = (
        null_vectors.shape[0],
        null_vectors.shape[2],
        null_vectors.shape[3],
        null_vectors.shape[4],
    )
    part = jnp.transpose(coarse_rounded, (3, 0, 1, 2))
    selector = block_matrix(plane).astype(jnp.bfloat16)
    spread = jnp.einsum("ktxc,pc->ktxp", part, selector, preferred_element_type=jnp.float32).astype(
        jnp.bfloat16
    )
    spread = jnp.broadcast_to(
        spread[:, :, None, :, None, :], (channels, depth // 4, 4, width // 4, 4, plane)
    )
    spread = spread.reshape(channels, depth, width, plane)
    return jnp.einsum("kmtxp,ktxp->mtxp", null_vectors, spread, preferred_element_type=jnp.float32)


def coarse_sweep(approx, coarse_rhs, inverse, couplings):
    padded = padded_2(approx, (("lat", 0), ("agg", 1)), 1)
    found = [padded[2:, 1:-1], padded[:-2, 1:-1], padded[1:-1, 2:], padded[1:-1, :-2]]
    grid = approx.reshape(approx.shape[0], approx.shape[1], CY // 4, CZ // 4, approx.shape[3])
    for axis in (2, 3):
        found.append(jnp.roll(grid, -1, axis).reshape(approx.shape))
        found.append(jnp.roll(grid, 1, axis).reshape(approx.shape))
    near = jnp.stack(found)
    off_terms = jnp.einsum("dpqskl,dpqsl->pqsk", couplings, near, precision=exact_mode)
    return jnp.einsum("pqskl,pqsl->pqsk", inverse, coarse_rhs - off_terms, precision=exact_mode)


def shards(solution, right_side, links, clover, null_vectors, coarse_inverse, coarse_links):
    residual = right_side - dirac(solution, links, clover)
    coarse_rhs = restrict(residual.astype(jnp.bfloat16), null_vectors)
    inverse = coarse_inverse.astype(jnp.float32)
    couplings = coarse_links.astype(jnp.float32)
    approx = jnp.einsum("pqskl,pqsl->pqsk", inverse, coarse_rhs, precision=exact_mode)
    for sweep in range(SWEEPS):
        approx = coarse_sweep(approx, coarse_rhs, inverse, couplings)
    updated = solution + prolong(approx.astype(jnp.bfloat16), null_vectors)
    return (updated, right_side - dirac(updated, links, clover))


def solution(mesh):
    placed = (
        P(None, "lat", "agg", None),
        P(None, "lat", "agg", None),
        P(None, None, None, "lat", "agg", None),
        P(None, None, None, "lat", "agg", None),
        P(None, None, "lat", "agg", None),
        P("lat", "agg", None, None, None),
        P(None, "lat", "agg", None, None, None),
    )
    return jax.shard_map(
        shards,
        mesh=mesh,
        in_specs=placed,
        out_specs=(P(None, "lat", "agg", None), P(None, "lat", "agg", None)),
        check_vma=False,
    )
```

profile of v0, /device:TPU:49, one launch (start us, length us, event | category | flops | bytes accessed | tf_op | source)
XLA Modules:
  0.0 103.8 jit_solution(12815139221853279463)
XLA Ops:
  0.6 0.9 slice_bitcast_fusion.37
  1.5 0.9 copy.37
  2.5 1.0 convert_element_type.26
  4.1 19.3 %collective-permute-start = (f32[36,1,4,128]{3,2,1,0:T(4,128)S(1)}, f32[36,1,4,128]{3,2,1,0:T(4,128)S(1)}, u32[]{:S(2)}, u32[]{:S(2)}) collective-permute-start(f32[36,1,4,128]{3,2,1,0:T(4,128)S(1)} %get-tuple-element.30), channel_id=1, source_target_pairs={{16,0},{32,16},{48,32},{64,48},{80,64},{96,80},{112,96},{128,112},... | collective-permute-start | bytes 221192 | tf_op jit(solution)/shard_map/ppermute | solution.py:25
  23.5 1.9 %collective-permute-start.1 = (f32[36,1,4,128]{3,2,1,0:T(4,128)S(1)}, f32[36,1,4,128]{3,2,1,0:T(4,128)S(1)}, u32[]{:S(2)}, u32[]{:S(2)}) collective-permute-start(f32[36,1,4,128]{3,2,1,0:T(4,128)S(1)} %get-tuple-element.31), channel_id=1, source_target_pairs={{0,16},{16,32},{32,48},{48,64},{64,80},{80,96},{96,112},{112,128},... | collective-permute-start | bytes 221192 | tf_op jit(solution)/shard_map/ppermute | solution.py:24
  26.1 0.4 fusion.14
  26.8 0.3 fusion.53
  27.4 4.5 %collective-permute-done.1 = f32[36,1,4,128]{3,2,1,0:T(4,128)S(1)} collective-permute-done((f32[36,1,4,128]{3,2,1,0:T(4,128)S(1)}, f32[36,1,4,128]{3,2,1,0:T(4,128)S(1)}, u32[]{:S(2)}, u32[]{:S(2)}) %collective-permute-start.1) | collective-permute-done | bytes 73760 | tf_op jit(solution)/shard_map/ppermute | solution.py:24
  32.1 4.6 %collective-permute-start.3 = (f32[36,6,1,128]{3,2,1,0:T(1,128)S(1)}, f32[36,6,1,128]{3,2,1,0:T(1,128)S(1)}, u32[]{:S(2)}, u32[]{:S(2)}) collective-permute-start(f32[36,6,1,128]{3,2,1,0:T(1,128)S(1)} %get-tuple-element.8), channel_id=1, source_target_pairs={{0,1},{1,2},{2,3},{3,4},{4,5},{5,6},{6,7},{7,8},{8,9},{9,10},{10,1... | collective-permute-start | bytes 331784 | tf_op jit(solution)/shard_map/ppermute | solution.py:24
  36.7 1.7 %collective-permute-done.3 = f32[36,6,1,128]{3,2,1,0:T(1,128)S(1)} collective-permute-done((f32[36,6,1,128]{3,2,1,0:T(1,128)S(1)}, f32[36,6,1,128]{3,2,1,0:T(1,128)S(1)}, u32[]{:S(2)}, u32[]{:S(2)}) %collective-permute-start.3) | collective-permute-done | bytes 110624 | tf_op jit(solution)/shard_map/ppermute | solution.py:24
  38.5 3.6 %collective-permute-done.2 = f32[36,6,1,128]{3,2,1,0:T(1,128)S(1)} collective-permute-done((f32[36,6,1,128]{3,2,1,0:T(1,128)S(1)}, f32[36,6,1,128]{3,2,1,0:T(1,128)S(1)}, u32[]{:S(2)}, u32[]{:S(2)}) %collective-permute-start.2) | collective-permute-done | bytes 110624 | tf_op jit(solution)/shard_map/ppermute | solution.py:25
  42.3 0.3 fusion.56
  42.6 0.3 fusion.59
  42.9 0.3 fusion.7
  43.3 0.3 fusion.6
  43.6 0.4 fusion.5
  44.2 0.6 fusion.8
  44.9 1.3 %multiply_reduce_fusion.1 = f32[128,48]{0,1:T(8,128)S(1)} fusion(f32[128,12,4,4]{0,3,2,1:T(4,128)S(1)} %bitcast_convert_fusion.1, bf16[48,12,4,4,128]{4,3,2,1,0:T(4,128)(2,1)S(1)} %copy-done.1), kind=kLoop, calls=%fused_computation.1 | loop fusion | flops 3532800 | bytes 2482176 | tf_op jit(solution)/shard_map/kmtxp,mtxp->ktxp/dot_general | solution.py:114
  46.7 1.9 %collective-permute-start.4 = (f32[1,1,8,48]{3,2,1,0:T(8,128)S(1)}, f32[1,1,8,48]{3,2,1,0:T(8,128)S(1)}, u32[]{:S(2)}, u32[]{:S(2)}) collective-permute-start(f32[1,1,8,48]{3,2,1,0:T(8,128)S(1)} %bitcast.444), channel_id=1, source_target_pairs={{16,0},{32,16},{48,32},{64,48},{80,64},{96,80},{112,96},{128,112},... | collective-permute-start | bytes 4616 | tf_op jit(solution)/shard_map/ppermute | solution.py:25
  48.7 3.4 %collective-permute-start.5 = (f32[1,1,8,48]{3,2,1,0:T(8,128)S(1)}, f32[1,1,8,48]{3,2,1,0:T(8,128)S(1)}, u32[]{:S(2)}, u32[]{:S(2)}) collective-permute-start(f32[1,1,8,48]{3,2,1,0:T(8,128)S(1)} %bitcast.445), channel_id=1, source_target_pairs={{0,16},{16,32},{32,48},{48,64},{64,80},{80,96},{96,112},{112,128},... | collective-permute-start | bytes 4616 | tf_op jit(solution)/shard_map/ppermute | solution.py:24
  52.1 4.2 %collective-permute-done.5 = f32[1,1,8,48]{3,2,1,0:T(8,128)S(1)} collective-permute-done((f32[1,1,8,48]{3,2,1,0:T(8,128)S(1)}, f32[1,1,8,48]{3,2,1,0:T(8,128)S(1)}, u32[]{:S(2)}, u32[]{:S(2)}) %collective-permute-start.5) | collective-permute-done | bytes 1568 | tf_op jit(solution)/shard_map/ppermute | solution.py:24
  56.3 3.0 %collective-permute-start.7 = (f32[3,1,8,48]{3,2,1,0:T(8,128)S(1)}, f32[3,1,8,48]{3,2,1,0:T(8,128)S(1)}, u32[]{:S(2)}, u32[]{:S(2)}) collective-permute-start(f32[3,1,8,48]{3,2,1,0:T(8,128)S(1)} %pad_maximum_fusion.24), channel_id=1, source_target_pairs={{0,1},{1,2},{2,3},{3,4},{4,5},{5,6},{6,7},{7,8},{8,9},{9,10},{10,1... | collective-permute-start | bytes 13832 | tf_op jit(solution)/shard_map/ppermute | solution.py:24
  59.3 1.4 %collective-permute-done.6 = f32[3,1,8,48]{3,2,1,0:T(8,128)S(1)} collective-permute-done((f32[3,1,8,48]{3,2,1,0:T(8,128)S(1)}, f32[3,1,8,48]{3,2,1,0:T(8,128)S(1)}, u32[]{:S(2)}, u32[]{:S(2)}) %collective-permute-start.6) | collective-permute-done | bytes 4640 | tf_op jit(solution)/shard_map/ppermute | solution.py:25
  60.7 0.7 fusion.12
  61.4 0.3 fusion.40
  61.7 1.9 %collective-permute-start.8 = (f32[1,1,8,48]{3,2,1,0:T(8,128)S(1)}, f32[1,1,8,48]{3,2,1,0:T(8,128)S(1)}, u32[]{:S(2)}, u32[]{:S(2)}) collective-permute-start(f32[1,1,8,48]{3,2,1,0:T(8,128)S(1)} %bitcast.438), channel_id=1, source_target_pairs={{16,0},{32,16},{48,32},{64,48},{80,64},{96,80},{112,96},{128,112},... | collective-permute-start | bytes 4616 | tf_op jit(solution)/shard_map/ppermute | solution.py:25
  63.6 3.4 %collective-permute-start.9 = (f32[1,1,8,48]{3,2,1,0:T(8,128)S(1)}, f32[1,1,8,48]{3,2,1,0:T(8,128)S(1)}, u32[]{:S(2)}, u32[]{:S(2)}) collective-permute-start(f32[1,1,8,48]{3,2,1,0:T(8,128)S(1)} %bitcast.439), channel_id=1, source_target_pairs={{0,16},{16,32},{32,48},{48,64},{64,80},{80,96},{96,112},{112,128},... | collective-permute-start | bytes 4616 | tf_op jit(solution)/shard_map/ppermute | solution.py:24
  67.1 4.2 %collective-permute-done.9 = f32[1,1,8,48]{3,2,1,0:T(8,128)S(1)} collective-permute-done((f32[1,1,8,48]{3,2,1,0:T(8,128)S(1)}, f32[1,1,8,48]{3,2,1,0:T(8,128)S(1)}, u32[]{:S(2)}, u32[]{:S(2)}) %collective-permute-start.9) | collective-permute-done | bytes 1568 | tf_op jit(solution)/shard_map/ppermute | solution.py:24
  71.3 4.1 %collective-permute-start.11 = (f32[3,1,8,48]{3,2,1,0:T(8,128)S(1)}, f32[3,1,8,48]{3,2,1,0:T(8,128)S(1)}, u32[]{:S(2)}, u32[]{:S(2)}) collective-permute-start(f32[3,1,8,48]{3,2,1,0:T(8,128)S(1)} %pad_maximum_fusion.25), channel_id=1, source_target_pairs={{0,1},{1,2},{2,3},{3,4},{4,5},{5,6},{6,7},{7,8},{8,9},{9,10},{10,1... | collective-permute-start | bytes 13832 | tf_op jit(solution)/shard_map/ppermute | solution.py:24
  75.5 1.4 %collective-permute-done.10 = f32[3,1,8,48]{3,2,1,0:T(8,128)S(1)} collective-permute-done((f32[3,1,8,48]{3,2,1,0:T(8,128)S(1)}, f32[3,1,8,48]{3,2,1,0:T(8,128)S(1)}, u32[]{:S(2)}, u32[]{:S(2)}) %collective-permute-start.10) | collective-permute-done | bytes 4640 | tf_op jit(solution)/shard_map/ppermute | solution.py:25
  76.9 0.7 fusion.10
  77.6 0.3 fusion.38
  78.2 1.3 %multiply_reduce_fusion = f32[4,4,128,12]{2,1,0,3:T(4,128)S(1)} fusion(f32[4,4,128,48]{2,1,0,3:T(4,128)S(1)} %bitcast_convert_fusion, bf16[48,12,4,4,128]{4,3,2,1,0:T(4,128)(2,1)S(1)} %copy-done.1), kind=kLoop, calls=%fused_computation | loop fusion | flops 3514368 | bytes 2850816 | tf_op jit(solution)/shard_map/kmtxp,ktxp->mtxp/dot_general | solution.py:137
  80.4 1.9 %collective-permute-start.12 = (f32[36,1,4,128]{3,2,1,0:T(4,128)S(1)}, f32[36,1,4,128]{3,2,1,0:T(4,128)S(1)}, u32[]{:S(2)}, u32[]{:S(2)}) collective-permute-start(f32[36,1,4,128]{3,2,1,0:T(4,128)S(1)} %get-tuple-element.14), channel_id=1, source_target_pairs={{16,0},{32,16},{48,32},{64,48},{80,64},{96,80},{112,96},{128,112},... | collective-permute-start | bytes 221192 | tf_op jit(solution)/shard_map/ppermute | solution.py:25
  82.4 3.5 %collective-permute-start.13 = (f32[36,1,4,128]{3,2,1,0:T(4,128)S(1)}, f32[36,1,4,128]{3,2,1,0:T(4,128)S(1)}, u32[]{:S(2)}, u32[]{:S(2)}) collective-permute-start(f32[36,1,4,128]{3,2,1,0:T(4,128)S(1)} %get-tuple-element.15), channel_id=1, source_target_pairs={{0,16},{16,32},{32,48},{48,64},{64,80},{80,96},{96,112},{112,128},... | collective-permute-start | bytes 221192 | tf_op jit(solution)/shard_map/ppermute | solution.py:24
  85.9 0.4 fusion.26
  86.5 0.3 fusion.45
  86.8 4.0 %collective-permute-done.13 = f32[36,1,4,128]{3,2,1,0:T(4,128)S(1)} collective-permute-done((f32[36,1,4,128]{3,2,1,0:T(4,128)S(1)}, f32[36,1,4,128]{3,2,1,0:T(4,128)S(1)}, u32[]{:S(2)}, u32[]{:S(2)}) %collective-permute-start.13) | collective-permute-done | bytes 73760 | tf_op jit(solution)/shard_map/ppermute | solution.py:24
  91.0 4.1 %collective-permute-start.15 = (f32[36,6,1,128]{3,2,1,0:T(1,128)S(1)}, f32[36,6,1,128]{3,2,1,0:T(1,128)S(1)}, u32[]{:S(2)}, u32[]{:S(2)}) collective-permute-start(f32[36,6,1,128]{3,2,1,0:T(1,128)S(1)} %get-tuple-element.4), channel_id=1, source_target_pairs={{0,1},{1,2},{2,3},{3,4},{4,5},{5,6},{6,7},{7,8},{8,9},{9,10},{10,1... | collective-permute-start | bytes 331784 | tf_op jit(solution)/shard_map/ppermute | solution.py:24
  95.5 1.3 %collective-permute-done.15 = f32[36,6,1,128]{3,2,1,0:T(1,128)S(1)} collective-permute-done((f32[36,6,1,128]{3,2,1,0:T(1,128)S(1)}, f32[36,6,1,128]{3,2,1,0:T(1,128)S(1)}, u32[]{:S(2)}, u32[]{:S(2)}) %collective-permute-start.15) | collective-permute-done | bytes 110624 | tf_op jit(solution)/shard_map/ppermute | solution.py:24
  96.8 3.6 %collective-permute-done.14 = f32[36,6,1,128]{3,2,1,0:T(1,128)S(1)} collective-permute-done((f32[36,6,1,128]{3,2,1,0:T(1,128)S(1)}, f32[36,6,1,128]{3,2,1,0:T(1,128)S(1)}, u32[]{:S(2)}, u32[]{:S(2)}) %collective-permute-start.14) | collective-permute-done | bytes 110624 | tf_op jit(solution)/shard_map/ppermute | solution.py:25
  100.6 0.3 fusion.48
  100.9 0.3 fusion.51
  101.2 0.4 fusion.3
  101.6 0.3 fusion.2
  101.9 0.4 fusion.1
  102.4 0.7 fusion.9
  103.1 0.7 bitcast_subtract_fusion
  (158 shorter events, 5.1 us)
Async XLA Ops:
  0.6 60.1 %copy-start = (bf16[8,1,1,8,48,48]{5,4,3,2,1,0:T(8,128)(2,1)S(1)}, bf16[8,1,1,8,48,48]{5,4,3,2,1,0:T(8,128)(2,1)}, u32[]{:S(2)}) copy-start(bf16[8,1,1,8,48,48]{5,4,3,2,1,0:T(8,128)(2,1)} %param.29) | copy-start | bytes 884740
  2.5 23.1 %copy-start.2 = (f32[12,4,4,128]{3,2,1,0:T(4,128)S(1)}, f32[12,4,4,128]{3,2,1,0:T(4,128)}, u32[]{:S(2)}) copy-start(f32[12,4,4,128]{3,2,1,0:T(4,128)} %param.23) | copy-start | bytes 294916
  3.5 22.5 %copy-start.12 = (f32[4,4,1,1,1]{1,0,4,3,2:T(4,128)S(1)}, f32[4,4,1,1,1]{1,0,4,3,2:T(4,128)}, u32[]{:S(2)}) copy-start(f32[4,4,1,1,1]{1,0,4,3,2:T(4,128)} %constant.118) | copy-start | bytes 196
  3.7 23.1 %copy-start.11 = (f32[4,4,1,1,1]{1,0,4,3,2:T(4,128)S(1)}, f32[4,4,1,1,1]{1,0,4,3,2:T(4,128)}, u32[]{:S(2)}) copy-start(f32[4,4,1,1,1]{1,0,4,3,2:T(4,128)} %constant.120) | copy-start | bytes 196
  3.9 23.2 %copy-start.4 = (bf16[2,6,6,4,4,128]{5,4,3,2,1,0:T(4,128)(2,1)S(1)}, bf16[2,6,6,4,4,128]{5,4,3,2,1,0:T(4,128)(2,1)}, u32[]{:S(2)}) copy-start(bf16[2,6,6,4,4,128]{5,4,3,2,1,0:T(4,128)(2,1)} %param.26) | copy-start | bytes 884740
  4.1 23.3 %collective-permute-start = (f32[36,1,4,128]{3,2,1,0:T(4,128)S(1)}, f32[36,1,4,128]{3,2,1,0:T(4,128)S(1)}, u32[]{:S(2)}, u32[]{:S(2)}) collective-permute-start(f32[36,1,4,128]{3,2,1,0:T(4,128)S(1)} %get-tuple-element.30), channel_id=1, source_target_pairs={{16,0},{32,16},{48,32},{64,48},{80,64},{96,80},{112,96},{128,112},... | collective-permute-start | bytes 221192 | tf_op jit(solution)/shard_map/ppermute | solution.py:25
  23.5 8.4 %collective-permute-start.1 = (f32[36,1,4,128]{3,2,1,0:T(4,128)S(1)}, f32[36,1,4,128]{3,2,1,0:T(4,128)S(1)}, u32[]{:S(2)}, u32[]{:S(2)}) collective-permute-start(f32[36,1,4,128]{3,2,1,0:T(4,128)S(1)} %get-tuple-element.31), channel_id=1, source_target_pairs={{0,16},{16,32},{32,48},{48,64},{64,80},{80,96},{96,112},{112,128},... | collective-permute-start | bytes 221192 | tf_op jit(solution)/shard_map/ppermute | solution.py:24
  26.6 15.7 %copy-start.10 = (f32[4,4,1,1,1]{1,0,4,3,2:T(4,128)S(1)}, f32[4,4,1,1,1]{1,0,4,3,2:T(4,128)}, u32[]{:S(2)}) copy-start(f32[4,4,1,1,1]{1,0,4,3,2:T(4,128)} %constant.116) | copy-start | bytes 196
  26.8 15.8 %copy-start.9 = (f32[4,4,1,1,1]{1,0,4,3,2:T(4,128)S(1)}, f32[4,4,1,1,1]{1,0,4,3,2:T(4,128)}, u32[]{:S(2)}) copy-start(f32[4,4,1,1,1]{1,0,4,3,2:T(4,128)} %constant.114) | copy-start | bytes 196
  27.1 15.8 %copy-start.14 = (f32[4,4,1,1,1]{1,0,4,3,2:T(4,128)S(1)}, f32[4,4,1,1,1]{1,0,4,3,2:T(4,128)}, u32[]{:S(2)}) copy-start(f32[4,4,1,1,1]{1,0,4,3,2:T(4,128)} %constant.115) | copy-start | bytes 196
  27.1 16.2 %copy-start.8 = (f32[4,4,1,1,1]{1,0,4,3,2:T(4,128)S(1)}, f32[4,4,1,1,1]{1,0,4,3,2:T(4,128)}, u32[]{:S(2)}) copy-start(f32[4,4,1,1,1]{1,0,4,3,2:T(4,128)} %constant.117) | copy-start | bytes 196
  27.2 16.4 %copy-start.7 = (f32[4,4,1,1,1]{1,0,4,3,2:T(4,128)S(1)}, f32[4,4,1,1,1]{1,0,4,3,2:T(4,128)}, u32[]{:S(2)}) copy-start(f32[4,4,1,1,1]{1,0,4,3,2:T(4,128)} %constant.119) | copy-start | bytes 196
  27.4 16.8 %copy-start.6 = (f32[4,4,1,1,1]{1,0,4,3,2:T(4,128)S(1)}, f32[4,4,1,1,1]{1,0,4,3,2:T(4,128)}, u32[]{:S(2)}) copy-start(f32[4,4,1,1,1]{1,0,4,3,2:T(4,128)} %constant.121) | copy-start | bytes 196
  32.1 6.4 %collective-permute-start.3 = (f32[36,6,1,128]{3,2,1,0:T(1,128)S(1)}, f32[36,6,1,128]{3,2,1,0:T(1,128)S(1)}, u32[]{:S(2)}, u32[]{:S(2)}) collective-permute-start(f32[36,6,1,128]{3,2,1,0:T(1,128)S(1)} %get-tuple-element.8), channel_id=1, source_target_pairs={{0,1},{1,2},{2,3},{3,4},{4,5},{5,6},{6,7},{7,8},{8,9},{9,10},{10,1... | collective-permute-start | bytes 331784 | tf_op jit(solution)/shard_map/ppermute | solution.py:24
  36.7 5.4 %collective-permute-start.2 = (f32[36,6,1,128]{3,2,1,0:T(1,128)S(1)}, f32[36,6,1,128]{3,2,1,0:T(1,128)S(1)}, u32[]{:S(2)}, u32[]{:S(2)}) collective-permute-start(f32[36,6,1,128]{3,2,1,0:T(1,128)S(1)} %get-tuple-element.9), channel_id=1, source_target_pairs={{1,0},{2,1},{3,2},{4,3},{5,4},{6,5},{7,6},{8,7},{9,8},{10,9},{11,1... | collective-permute-start | bytes 331784 | tf_op jit(solution)/shard_map/ppermute | solution.py:25
  42.2 2.6 %copy-start.5 = (f32[12,4,4,128]{3,2,1,0:T(4,128)S(1)}, f32[12,4,4,128]{3,2,1,0:T(4,128)}, u32[]{:S(2)}) copy-start(f32[12,4,4,128]{3,2,1,0:T(4,128)} %param.24) | copy-start | bytes 294916
  42.3 2.6 %copy-start.1 = (bf16[48,12,4,4,128]{4,3,2,1,0:T(4,128)(2,1)S(1)}, bf16[48,12,4,4,128]{4,3,2,1,0:T(4,128)(2,1)}, u32[]{:S(2)}) copy-start(bf16[48,12,4,4,128]{4,3,2,1,0:T(4,128)(2,1)} %param.27) | copy-start | bytes 7077892
  44.1 2.4 %copy-start.13 = (bf16[1,1,8,48,48]{4,3,2,1,0:T(8,128)(2,1)S(1)}, bf16[1,1,8,48,48]{4,3,2,1,0:T(8,128)(2,1)}, u32[]{:S(2)}) copy-start(bf16[1,1,8,48,48]{4,3,2,1,0:T(8,128)(2,1)} %param.28) | copy-start | bytes 110596
  46.7 5.4 %collective-permute-start.4 = (f32[1,1,8,48]{3,2,1,0:T(8,128)S(1)}, f32[1,1,8,48]{3,2,1,0:T(8,128)S(1)}, u32[]{:S(2)}, u32[]{:S(2)}) collective-permute-start(f32[1,1,8,48]{3,2,1,0:T(8,128)S(1)} %bitcast.444), channel_id=1, source_target_pairs={{16,0},{32,16},{48,32},{64,48},{80,64},{96,80},{112,96},{128,112},... | collective-permute-start | bytes 4616 | tf_op jit(solution)/shard_map/ppermute | solution.py:25
  48.7 7.7 %collective-permute-start.5 = (f32[1,1,8,48]{3,2,1,0:T(8,128)S(1)}, f32[1,1,8,48]{3,2,1,0:T(8,128)S(1)}, u32[]{:S(2)}, u32[]{:S(2)}) collective-permute-start(f32[1,1,8,48]{3,2,1,0:T(8,128)S(1)} %bitcast.445), channel_id=1, source_target_pairs={{0,16},{16,32},{32,48},{48,64},{64,80},{80,96},{96,112},{112,128},... | collective-permute-start | bytes 4616 | tf_op jit(solution)/shard_map/ppermute | solution.py:24
  56.3 4.3 %collective-permute-start.6 = (f32[3,1,8,48]{3,2,1,0:T(8,128)S(1)}, f32[3,1,8,48]{3,2,1,0:T(8,128)S(1)}, u32[]{:S(2)}, u32[]{:S(2)}) collective-permute-start(f32[3,1,8,48]{3,2,1,0:T(8,128)S(1)} %pad_maximum_fusion.24), channel_id=1, source_target_pairs={{1,0},{2,1},{3,2},{4,3},{5,4},{6,5},{7,6},{8,7},{9,8},{10,9},{11,1... | collective-permute-start | bytes 13832 | tf_op jit(solution)/shard_map/ppermute | solution.py:25
  56.3 4.3 %collective-permute-start.7 = (f32[3,1,8,48]{3,2,1,0:T(8,128)S(1)}, f32[3,1,8,48]{3,2,1,0:T(8,128)S(1)}, u32[]{:S(2)}, u32[]{:S(2)}) collective-permute-start(f32[3,1,8,48]{3,2,1,0:T(8,128)S(1)} %pad_maximum_fusion.24), channel_id=1, source_target_pairs={{0,1},{1,2},{2,3},{3,4},{4,5},{5,6},{6,7},{7,8},{8,9},{9,10},{10,1... | collective-permute-start | bytes 13832 | tf_op jit(solution)/shard_map/ppermute | solution.py:24
  61.7 5.4 %collective-permute-start.8 = (f32[1,1,8,48]{3,2,1,0:T(8,128)S(1)}, f32[1,1,8,48]{3,2,1,0:T(8,128)S(1)}, u32[]{:S(2)}, u32[]{:S(2)}) collective-permute-start(f32[1,1,8,48]{3,2,1,0:T(8,128)S(1)} %bitcast.438), channel_id=1, source_target_pairs={{16,0},{32,16},{48,32},{64,48},{80,64},{96,80},{112,96},{128,112},... | collective-permute-start | bytes 4616 | tf_op jit(solution)/shard_map/ppermute | solution.py:25
  63.6 7.7 %collective-permute-start.9 = (f32[1,1,8,48]{3,2,1,0:T(8,128)S(1)}, f32[1,1,8,48]{3,2,1,0:T(8,128)S(1)}, u32[]{:S(2)}, u32[]{:S(2)}) collective-permute-start(f32[1,1,8,48]{3,2,1,0:T(8,128)S(1)} %bitcast.439), channel_id=1, source_target_pairs={{0,16},{16,32},{32,48},{48,64},{64,80},{80,96},{96,112},{112,128},... | collective-permute-start | bytes 4616 | tf_op jit(solution)/shard_map/ppermute | solution.py:24
  71.3 5.5 %collective-permute-start.10 = (f32[3,1,8,48]{3,2,1,0:T(8,128)S(1)}, f32[3,1,8,48]{3,2,1,0:T(8,128)S(1)}, u32[]{:S(2)}, u32[]{:S(2)}) collective-permute-start(f32[3,1,8,48]{3,2,1,0:T(8,128)S(1)} %pad_maximum_fusion.25), channel_id=1, source_target_pairs={{1,0},{2,1},{3,2},{4,3},{5,4},{6,5},{7,6},{8,7},{9,8},{10,9},{11,1... | collective-permute-start | bytes 13832 | tf_op jit(solution)/shard_map/ppermute | solution.py:25
  71.3 5.5 %collective-permute-start.11 = (f32[3,1,8,48]{3,2,1,0:T(8,128)S(1)}, f32[3,1,8,48]{3,2,1,0:T(8,128)S(1)}, u32[]{:S(2)}, u32[]{:S(2)}) collective-permute-start(f32[3,1,8,48]{3,2,1,0:T(8,128)S(1)} %pad_maximum_fusion.25), channel_id=1, source_target_pairs={{0,1},{1,2},{2,3},{3,4},{4,5},{5,6},{6,7},{7,8},{8,9},{9,10},{10,1... | collective-permute-start | bytes 13832 | tf_op jit(solution)/shard_map/ppermute | solution.py:24
  79.5 23.0 %copy-start.3 = (f32[12,4,4,128]{3,2,1,0:T(4,128)}, f32[12,4,4,128]{3,2,1,0:T(4,128)S(1)}, u32[]{:S(2)}) copy-start(f32[12,4,4,128]{3,2,1,0:T(4,128)S(1)} %bitcast_add_fusion) | copy-start | bytes 294916
  80.4 6.4 %collective-permute-start.12 = (f32[36,1,4,128]{3,2,1,0:T(4,128)S(1)}, f32[36,1,4,128]{3,2,1,0:T(4,128)S(1)}, u32[]{:S(2)}, u32[]{:S(2)}) collective-permute-start(f32[36,1,4,128]{3,2,1,0:T(4,128)S(1)} %get-tuple-element.14), channel_id=1, source_target_pairs={{16,0},{32,16},{48,32},{64,48},{80,64},{96,80},{112,96},{128,112},... | collective-permute-start | bytes 221192 | tf_op jit(solution)/shard_map/ppermute | solution.py:25
  82.4 8.4 %collective-permute-start.13 = (f32[36,1,4,128]{3,2,1,0:T(4,128)S(1)}, f32[36,1,4,128]{3,2,1,0:T(4,128)S(1)}, u32[]{:S(2)}, u32[]{:S(2)}) collective-permute-start(f32[36,1,4,128]{3,2,1,0:T(4,128)S(1)} %get-tuple-element.15), channel_id=1, source_target_pairs={{0,16},{16,32},{32,48},{48,64},{64,80},{80,96},{96,112},{112,128},... | collective-permute-start | bytes 221192 | tf_op jit(solution)/shard_map/ppermute | solution.py:24
  91.0 5.9 %collective-permute-start.15 = (f32[36,6,1,128]{3,2,1,0:T(1,128)S(1)}, f32[36,6,1,128]{3,2,1,0:T(1,128)S(1)}, u32[]{:S(2)}, u32[]{:S(2)}) collective-permute-start(f32[36,6,1,128]{3,2,1,0:T(1,128)S(1)} %get-tuple-element.4), channel_id=1, source_target_pairs={{0,1},{1,2},{2,3},{3,4},{4,5},{5,6},{6,7},{7,8},{8,9},{9,10},{10,1... | collective-permute-start | bytes 331784 | tf_op jit(solution)/shard_map/ppermute | solution.py:24
  95.1 5.4 %collective-permute-start.14 = (f32[36,6,1,128]{3,2,1,0:T(1,128)S(1)}, f32[36,6,1,128]{3,2,1,0:T(1,128)S(1)}, u32[]{:S(2)}, u32[]{:S(2)}) collective-permute-start(f32[36,6,1,128]{3,2,1,0:T(1,128)S(1)} %get-tuple-element.5), channel_id=1, source_target_pairs={{1,0},{2,1},{3,2},{4,3},{5,4},{6,5},{7,6},{8,7},{9,8},{10,9},{11,1... | collective-permute-start | bytes 331784 | tf_op jit(solution)/shard_map/ppermute | solution.py:25
where the time goes:
time: 104 us
  starting transfers between devices  53.1 us (51%)
  waiting for transfers between devices  29.9 us (29%)
  matrix products  8.64 us (8%)
  other arithmetic  5.96 us (6%)
  local copies, waits for them, and re-layouts  4.34 us (4%)
  between operations  1.83 us (2%)
    ppermute x8, starting transfers between devices, padded_2(): before = lax.ppermute(last, axis, up)  28 us
    ppermute x8, starting transfers between devices, padded_2(): after = lax.ppermute(leading, axis, down)  25.2 us
    ppermute x8, waiting for transfers between devices, padded_2(): before = lax.ppermute(last, axis, up)  19.9 us
    ppermute x8, waiting for transfers between devices, padded_2(): after = lax.ppermute(leading, axis, down)  9.99 us
    dot_general x16, matrix products, spin_apply(): jnp.einsum('st,t...->s...', jnp.asarray(matrix, spinor.dtype), spinor, pr...  5.93 us
  transfers between devices with their start and end apart: 16, of which 10 were waited for; matrix products, arithmetic and copies ran while one was open for 3% of the time, Pallas kernels for 0%

commit v1 on v0

v1 whole, which is shorter than its diff:
```python
import jax
import jax.numpy as jnp
from jax import lax
from jax.experimental import pallas as pl
from jax.experimental.pallas import tpu as pltpu
from jax.sharding import PartitionSpec as P

CY = 8
CZ = 16
SWEEPS = 2
ROWS = 16
LANES = 128
FACE = 4
SPAN = 4

exact_mode = lax.Precision.HIGHEST
hopping = 0.5
wilson_mass = 4.0

VMEM = pl.BlockSpec(memory_space=pltpu.VMEM)
LIMIT = 24 * 1024 * 1024

EXPAND = {
    (0, 1): ((0, 0, 1), (1, 1, 1), (2, 0, -1), (3, 1, -1)),
    (0, -1): ((0, 0, 1), (1, 1, 1), (2, 0, 1), (3, 1, 1)),
    (1, 1): ((0, 0, 1), (3, 0, -1), (1, 1, 1), (2, 1, -1)),
    (1, -1): ((0, 0, 1), (3, 0, 1), (1, 1, 1), (2, 1, 1)),
    (2, 1): ((2, 0, 1), (3, 1, 1)),
    (2, -1): ((0, 0, 1), (1, 1, 1)),
    (3, 1): ((0, 0, 1), (1, 0, -1), (2, 1, 1), (3, 1, 1)),
    (3, -1): ((0, 0, 1), (1, 0, 1), (2, 1, 1), (3, 1, -1)),
}


def half(v, axis, direction):
    def mix(a, b, sign):
        return [v[a * 3 + c] + v[b * 3 + c] if sign > 0 else v[a * 3 + c] - v[b * 3 + c] for c in range(3)]

    if axis == 0:
        return mix(0, 2, -direction) + mix(1, 3, -direction)
    if axis == 1:
        return mix(0, 3, -direction) + mix(1, 2, -direction)
    if axis == 2:
        first = 2 if direction == 1 else 0
        return [2.0 * v[first * 3 + c] for c in range(6)]
    return mix(0, 1, -direction) + mix(2, 3, direction)


def transport(links_ref, axis, h, transposed):
    found = [None] * 6
    for i in range(3):
        for j in range(3):
            u = links_ref[axis * 9 + (j * 3 + i if transposed else i * 3 + j)].astype(jnp.float32)
            for spin in range(2):
                term = u * h[spin * 3 + j]
                at = spin * 3 + i
                found[at] = term if found[at] is None else found[at] + term
    return found


def place(dim):
    return lax.broadcasted_iota(jnp.int32, (ROWS, LANES), dim)


def shifted(value, axis, direction, halo):
    if axis == 0:
        moved = pltpu.roll(value, (-direction * FACE) % ROWS, 0)
        edge = ROWS // FACE - 1 if direction == 1 else 0
        return jnp.where(place(0) // FACE == edge, halo, moved)
    if axis == 1:
        moved = pltpu.roll(value, (-direction) % ROWS, 0)
        edge = FACE - 1 if direction == 1 else 0
        return jnp.where(place(0) % FACE == edge, halo, moved)
    if axis == 2:
        return pltpu.roll(value, (-direction * CZ) % LANES, 1)
    inside = pltpu.roll(value, (-direction) % LANES, 1)
    wrapped = pltpu.roll(value, (direction * (CZ - 1)) % LANES, 1)
    edge = CZ - 1 if direction == 1 else 0
    return jnp.where(place(1) % CZ == edge, wrapped, inside)


def halo_tile(halo_ref, axis, c):
    face = halo_ref[c * FACE : (c + 1) * FACE, :]
    if axis == 0:
        return jnp.concatenate([face] * (ROWS // FACE), axis=0)
    tile = jnp.broadcast_to(face[0:1], (ROWS, LANES))
    for t in range(1, FACE):
        tile = jnp.where(place(0) // FACE == t, jnp.broadcast_to(face[t : t + 1], (ROWS, LANES)), tile)
    return tile


def dirac(v, links_ref, clover_ref, halos):
    hops = [None] * 12
    for axis in range(4):
        for direction in (1, -1):
            h = half(v, axis, direction)
            if direction == -1:
                h = transport(links_ref, axis, h, True)
            near = []
            for c in range(6):
                halo = halo_tile(halos[axis, direction], axis, c) if axis < 2 else None
                near.append(shifted(h[c], axis, direction, halo))
            if direction == 1:
                near = transport(links_ref, axis, near, False)
            for spin, part, sign in EXPAND[axis, direction]:
                for c in range(3):
                    at, term = spin * 3 + c, near[part * 3 + c]
                    if hops[at] is None:
                        hops[at] = term if sign > 0 else -term
                    else:
                        hops[at] = hops[at] + term if sign > 0 else hops[at] - term
    total = []
    for block in range(2):
        for i in range(6):
            local = None
            for j in range(6):
                term = clover_ref[(block * 6 + i) * 6 + j].astype(jnp.float32) * v[block * 6 + j]
                local = term if local is None else local + term
            at = block * 6 + i
            total.append(wilson_mass * v[at] + local - hopping * hops[at])
    return total


def write_faces(v, links_ref, faces, work_ref):
    t_up, t_down, x_up, x_down = faces
    back = transport(links_ref, 0, half(v, 0, -1), True)
    ahead = half(v, 0, 1)
    for c in range(6):
        t_up[c * FACE : (c + 1) * FACE, :] = back[c][ROWS - FACE :]
        t_down[c * FACE : (c + 1) * FACE, :] = ahead[c][:FACE]
    back = transport(links_ref, 1, half(v, 1, -1), True)
    ahead = half(v, 1, 1)
    for c in range(6):
        work_ref[c] = back[c]
        work_ref[6 + c] = ahead[c]
    for c in range(6):
        x_up[c * FACE : (c + 1) * FACE, :] = work_ref[c, pl.ds(FACE - 1, FACE, stride=FACE), :]
        x_down[c * FACE : (c + 1) * FACE, :] = work_ref[6 + c, pl.ds(0, FACE, stride=FACE), :]


def faces_kernel(field_ref, links_ref, t_up, t_down, x_up, x_down, work_ref):
    write_faces([field_ref[m] for m in range(12)], links_ref, (t_up, t_down, x_up, x_down), work_ref)


def residual_tiles(field_ref, right_ref, links_ref, clover_ref, t_back, t_ahead, x_back, x_ahead):
    halos = {(0, -1): t_back, (0, 1): t_ahead, (1, -1): x_back, (1, 1): x_ahead}
    total = dirac([field_ref[m] for m in range(12)], links_ref, clover_ref, halos)
    return [right_ref[m] - total[m] for m in range(12)]


def owner_table(blocks):
    places = lax.broadcasted_iota(jnp.int32, (blocks, LANES), 1)
    owners = places // (CZ * SPAN) * (CZ // SPAN) + places % CZ // SPAN
    return owners == lax.broadcasted_iota(jnp.int32, (blocks, LANES), 0)


def restrict_kernel(
    field_ref, right_ref, links_ref, clover_ref, t_back, t_ahead, x_back, x_ahead, null_ref, coarse_ref, summed_ref
):
    residual = residual_tiles(field_ref, right_ref, links_ref, clover_ref, t_back, t_ahead, x_back, x_ahead)
    rough = [r.astype(jnp.bfloat16).astype(jnp.float32) for r in residual]
    channels = summed_ref.shape[0]

    def one(k, _):
        total = None
        for m in range(12):
            term = null_ref[k * 12 + m].astype(jnp.float32) * rough[m]
            total = term if total is None else total + term
        summed_ref[pl.ds(k, 1), :] = jnp.sum(total, axis=0, keepdims=True)
        return 0

    lax.fori_loop(0, channels, one, 0, unroll=4)
    table = owner_table(coarse_ref.shape[0]).astype(jnp.float32)
    coarse_ref[...] = lax.dot_general(
        table, summed_ref[...], (((1,), (1,)), ((), ())), precision=exact_mode, preferred_element_type=jnp.float32
    )


def prolong_kernel(
    field_ref, links_ref, null_ref, approx_ref, updated_ref, t_up, t_down, x_up, x_down, spread_ref, work_ref
):
    channels, blocks = approx_ref.shape
    table = owner_table(blocks).astype(jnp.bfloat16)
    spread_ref[...] = jnp.dot(approx_ref[...].astype(jnp.bfloat16), table, preferred_element_type=jnp.float32)

    def one(k, totals):
        row = jnp.broadcast_to(spread_ref[pl.ds(k, 1), :], (ROWS, LANES))
        return tuple(totals[m] + null_ref[k * 12 + m].astype(jnp.float32) * row for m in range(12))

    start = tuple(jnp.zeros((ROWS, LANES), jnp.float32) for _ in range(12))
    added = lax.fori_loop(0, channels, one, start, unroll=4)
    updated = [field_ref[m] + added[m] for m in range(12)]
    for m in range(12):
        updated_ref[m] = updated[m]
    write_faces(updated, links_ref, (t_up, t_down, x_up, x_down), work_ref)


def residual_kernel(field_ref, right_ref, links_ref, clover_ref, t_back, t_ahead, x_back, x_ahead, out_ref):
    residual = residual_tiles(field_ref, right_ref, links_ref, clover_ref, t_back, t_ahead, x_back, x_ahead)
    for m in range(12):
        out_ref[m] = residual[m]


def call(kernel, outs, scratch, *args):
    return pl.pallas_call(
        kernel,
        out_shape=[jax.ShapeDtypeStruct(shape, jnp.float32) for shape in outs],
        in_specs=[VMEM] * len(args),
        out_specs=[VMEM] * len(outs),
        scratch_shapes=[pltpu.VMEM(shape, jnp.float32) for shape in scratch],
        compiler_params=pltpu.CompilerParams(vmem_limit_bytes=LIMIT),
    )(*args)


def moved(value, axis, step):
    size = lax.axis_size(axis)
    return lax.ppermute(value, axis, [(i, (i + step) % size) for i in range(size)])


def swap_faces(faces):
    t_up, t_down, x_up, x_down = faces
    return moved(t_up, "lat", 1), moved(t_down, "lat", -1), moved(x_up, "agg", 1), moved(x_down, "agg", -1)


def coarse_sweep(approx, coarse_rhs, inverse, couplings):
    grid = approx.reshape(CY // SPAN, CZ // SPAN, approx.shape[1])
    near = [moved(approx, "lat", -1), moved(approx, "lat", 1), moved(approx, "agg", -1), moved(approx, "agg", 1)]
    for axis in (0, 1):
        near.append(jnp.roll(grid, -1, axis).reshape(approx.shape))
        near.append(jnp.roll(grid, 1, axis).reshape(approx.shape))
    off_terms = jnp.einsum("dskl,dsl->sk", couplings, jnp.stack(near), precision=exact_mode)
    return jnp.einsum("skl,sl->sk", inverse, coarse_rhs - off_terms, precision=exact_mode)


def shards(solution, right_side, links, clover, null_vectors, coarse_inverse, coarse_links):
    shape = solution.shape
    tiles = (12, ROWS, LANES)
    field, right = solution.reshape(tiles), right_side.reshape(tiles)
    link_tiles = links.reshape(36, ROWS, LANES)
    clover_tiles = clover.reshape(72, ROWS, LANES)
    channels, blocks = coarse_inverse.shape[-1], coarse_inverse.shape[2]
    null_tiles = null_vectors.reshape(channels * 12, ROWS, LANES)
    inverse = coarse_inverse.astype(jnp.float32).reshape(blocks, channels, channels)
    couplings = coarse_links.astype(jnp.float32).reshape(8, blocks, channels, channels)
    face = (6 * FACE, LANES)

    halos = swap_faces(call(faces_kernel, [face] * 4, [tiles], field, link_tiles))
    (coarse_rhs,) = call(
        restrict_kernel,
        [(blocks, channels)],
        [(channels, LANES)],
        field,
        right,
        link_tiles,
        clover_tiles,
        *halos,
        null_tiles,
    )
    approx = jnp.einsum("skl,sl->sk", inverse, coarse_rhs, precision=exact_mode)
    for _ in range(SWEEPS):
        approx = coarse_sweep(approx, coarse_rhs, inverse, couplings)
    updated, *faces = call(
        prolong_kernel,
        [tiles] + [face] * 4,
        [(channels, LANES), tiles],
        field,
        link_tiles,
        null_tiles,
        approx.T,
    )
    halos = swap_faces(faces)
    (after,) = call(residual_kernel, [tiles], [], updated, right, link_tiles, clover_tiles, *halos)
    return updated.reshape(shape), after.reshape(shape)


def solution(mesh):
    placed = (
        P(None, "lat", "agg", None),
        P(None, "lat", "agg", None),
        P(None, None, None, "lat", "agg", None),
        P(None, None, None, "lat", "agg", None),
        P(None, None, "lat", "agg", None),
        P("lat", "agg", None, None, None),
        P(None, "lat", "agg", None, None, None),
    )
    return jax.shard_map(
        shards,
        mesh=mesh,
        in_specs=placed,
        out_specs=(P(None, "lat", "agg", None), P(None, "lat", "agg", None)),
        check_vma=False,
    )
```

time: 104 us -> 83.1 us (0.80)
  waiting for transfers between devices: 29.9 us -> 10.1 us
  starting transfers between devices: 53.1 us -> 59.8 us
  matrix products: 8.64 us -> 2.2 us
  other arithmetic: 5.96 us -> 0.05 us
  Pallas kernels: 0 us -> 2.89 us
  local copies, waits for them, and re-layouts: 4.34 us -> 6.52 us
    ppermute x16, waiting for transfers between devices: 29.9 us -> 10.1 us  [moved(): lax.ppermute(value, axis, [(i, (i + step) % size) for i in range(size)])]
    ppermute x16, starting transfers between devices: 53.1 us -> 59.8 us  [moved(): lax.ppermute(value, axis, [(i, (i + step) % size) for i in range(size)])]
    dot_general x23 -> x5, matrix products: 8.64 us -> 2.2 us  [the longest x2 1.4 us: coarse_sweep(): jnp.einsum('dskl,dsl->sk', couplings, jnp.stack(near), precision=exact_mode)]
    unnamed x44 -> x40, local copies, waits for them, and re-layouts: 0.13 us -> 6.37 us
    pallas_call x0 -> x4, Pallas kernels: none -> 2.89 us  [call(): pl.pallas_call(kernel, out_shape=[jax.ShapeDtypeStruct(shape, jnp.float32...]
    dot_general x2 -> x0, other arithmetic: 2.54 us -> none  [the longest x1 1.28 us: prolong(): jnp.einsum('kmtxp,ktxp->mtxp', null_vectors, spread, preferred_element_ty...]
    mul x47 -> x0, local copies, waits for them, and re-layouts: 1.42 us -> none  [the longest x17 1.06 us: color_apply(): total = transport[None, :, 0] * spinor[:, None, 0]]
    slice x21 -> x6, local copies, waits for them, and re-layouts: 1.44 us -> 0.05 us  [the longest x4 0.04 us: coarse_sweep(): near.append(jnp.roll(grid, 1, axis).reshape(approx.shape))]
  transfers between devices with their start and end apart: 16 -> 16, of which waited for: 10 -> 6; matrix products, arithmetic and copies ran while one was open for 3% -> 0% of each run, Pallas kernels for 0% -> 0%
where the time goes in v1:
time: 83.1 us; the launch traced here: 82.5 us
  starting transfers between devices  59.8 us (72%)
  waiting for transfers between devices  10.1 us (12%)
  local copies, waits for them, and re-layouts  6.52 us (8%)
  Pallas kernels  2.89 us (3%)
  matrix products  2.2 us (3%)
  between operations  0.97 us (1%)
    ppermute x16, starting transfers between devices, moved(): lax.ppermute(value, axis, [(i, (i + step) % size) for i in range(size)])  59.8 us
    ppermute x16, waiting for transfers between devices, moved(): lax.ppermute(value, axis, [(i, (i + step) % size) for i in range(size)])  10.1 us
    unnamed x40, local copies, waits for them, and re-layouts  6.37 us
    pallas_call x4, Pallas kernels, call(): pl.pallas_call(kernel, out_shape=[jax.ShapeDtypeStruct(shape, jnp.float32...  2.89 us
  transfers between devices with their start and end apart: 16, of which 6 were waited for; matrix products, arithmetic and copies ran while one was open for 0% of the time, Pallas kernels for 0%

profile of v1, /device:TPU:49, one launch (start us, length us, event | category | flops | bytes accessed | tf_op | source)
XLA Modules:
  0.0 82.5 jit_solution(15026308988028260522)
XLA Ops:
  0.6 0.0 copy-start
  0.6 0.0 copy-start.3
  0.7 1.0 %copy-done.3 = bf16[4,3,3,4,4,128]{5,4,3,2,1,0:T(4,128)(2,1)S(1)} copy-done((bf16[4,3,3,4,4,128]{5,4,3,2,1,0:T(4,128)(2,1)S(1)}, bf16[4,3,3,4,4,128]{5,4,3,2,1,0:T(4,128)(2,1)}, u32[]{:S(2)}) %copy-start.3) | copy-done | bytes 147480
  1.6 0.9 %copy-done.7 = f32[12,4,4,128]{3,2,1,0:T(4,128)S(1)} copy-done((f32[12,4,4,128]{3,2,1,0:T(4,128)S(1)}, f32[12,4,4,128]{3,2,1,0:T(4,128)}, u32[]{:S(2)}) %copy-start.7) | copy-done | bytes 98328
  2.6 4.9 %collective-permute-start = (f32[24,128]{1,0:T(8,128)S(1)}, f32[24,128]{1,0:T(8,128)S(1)}, u32[]{:S(2)}, u32[]{:S(2)}) collective-permute-start(f32[24,128]{1,0:T(8,128)S(1)} %get-tuple-element.11), channel_id=1, source_target_pairs={{0,16},{16,32},{32,48},{48,64},{64,80},{80,96},{96,112},{112,128},... | collective-permute-start | bytes 36872 | tf_op jit(solution)/shard_map/ppermute | solution.py:217
  7.5 16.4 %collective-permute-start.1 = (f32[24,128]{1,0:T(8,128)S(1)}, f32[24,128]{1,0:T(8,128)S(1)}, u32[]{:S(2)}, u32[]{:S(2)}) collective-permute-start(f32[24,128]{1,0:T(8,128)S(1)} %get-tuple-element.12), channel_id=1, source_target_pairs={{0,1008},{16,0},{32,16},{48,32},{64,48},{80,64},{96,80},{112,96},{... | collective-permute-start | bytes 36872 | tf_op jit(solution)/shard_map/ppermute | solution.py:217
  23.8 3.5 %collective-permute-start.2 = (f32[24,128]{1,0:T(8,128)S(1)}, f32[24,128]{1,0:T(8,128)S(1)}, u32[]{:S(2)}, u32[]{:S(2)}) collective-permute-start(f32[24,128]{1,0:T(8,128)S(1)} %get-tuple-element.13), channel_id=1, source_target_pairs={{0,1},{1,2},{2,3},{3,4},{4,5},{5,6},{6,7},{7,8},{8,9},{9,10},{10,1... | collective-permute-start | bytes 36872 | tf_op jit(solution)/shard_map/ppermute | solution.py:217
  27.3 0.0 collective-permute-start.3
  27.3 0.0 collective-permute-done.t_back
  27.3 0.0 collective-permute-done.1.t_ahead
  27.3 0.8 collective-permute-done.2.x_back
  28.1 3.5 %collective-permute-done.3.x_ahead = f32[24,128]{1,0:T(8,128)S(1)} collective-permute-done((f32[24,128]{1,0:T(8,128)S(1)}, f32[24,128]{1,0:T(8,128)S(1)}, u32[]{:S(2)}, u32[]{:S(2)}) %collective-permute-start.3) | collective-permute-done | bytes 12320 | tf_op jit(solution)/shard_map/ppermute | solution.py:217
  31.6 1.7 %copy-done.1 = bf16[48,12,4,4,128]{4,3,2,1,0:T(4,128)(2,1)S(1)} copy-done((bf16[48,12,4,4,128]{4,3,2,1,0:T(4,128)(2,1)S(1)}, bf16[48,12,4,4,128]{4,3,2,1,0:T(4,128)(2,1)}, u32[]{:S(2)}) %copy-start.1) | copy-done | bytes 2359320
  33.3 1.0 %copy-done.5 = bf16[2,6,6,4,4,128]{5,4,3,2,1,0:T(4,128)(2,1)S(1)} copy-done((bf16[2,6,6,4,4,128]{5,4,3,2,1,0:T(4,128)(2,1)S(1)}, bf16[2,6,6,4,4,128]{5,4,3,2,1,0:T(4,128)(2,1)}, u32[]{:S(2)}) %copy-start.5) | copy-done | bytes 294936
  34.3 0.9 %copy-done.9 = f32[12,4,4,128]{3,2,1,0:T(4,128)S(1)} copy-done((f32[12,4,4,128]{3,2,1,0:T(4,128)S(1)}, f32[12,4,4,128]{3,2,1,0:T(4,128)}, u32[]{:S(2)}) %copy-start.9) | copy-done | bytes 98328
  35.2 0.7 shard_map.87
  35.8 0.3 fusion.8
  36.1 0.0 collective-permute-start.7
  36.2 0.5 collective-permute-start.6
  36.7 1.9 %collective-permute-start.5 = (f32[8,48]{1,0:T(8,128)S(1)}, f32[8,48]{1,0:T(8,128)S(1)}, u32[]{:S(2)}, u32[]{:S(2)}) collective-permute-start(f32[8,48]{1,0:T(8,128)S(1)} %bitcast.120), channel_id=1, source_target_pairs={{0,16},{16,32},{32,48},{48,64},{64,80},{80,96},{96,112},{112,128},... | collective-permute-start | bytes 4616 | tf_op jit(solution)/shard_map/ppermute | solution.py:217
  38.6 6.7 %collective-permute-start.4 = (f32[8,48]{1,0:T(8,128)S(1)}, f32[8,48]{1,0:T(8,128)S(1)}, u32[]{:S(2)}, u32[]{:S(2)}) collective-permute-start(f32[8,48]{1,0:T(8,128)S(1)} %bitcast.121), channel_id=1, source_target_pairs={{0,1008},{16,0},{32,16},{48,32},{64,48},{80,64},{96,80},{112,96},{... | collective-permute-start | bytes 4616 | tf_op jit(solution)/shard_map/ppermute | solution.py:217
  45.3 0.7 collective-permute-done.4
  46.0 0.0 collective-permute-done.5
  46.0 0.0 collective-permute-done.6
  46.0 0.0 collective-permute-done.7
  46.1 0.0 copy-start.10
  46.1 0.7 fusion.2
  46.8 0.3 fusion.6
  47.1 3.6 %collective-permute-start.11 = (f32[8,48]{1,0:T(8,128)S(1)}, f32[8,48]{1,0:T(8,128)S(1)}, u32[]{:S(2)}, u32[]{:S(2)}) collective-permute-start(f32[8,48]{1,0:T(8,128)S(1)} %bitcast.125), channel_id=1, source_target_pairs={{0,1},{1,2},{2,3},{3,4},{4,5},{5,6},{6,7},{7,8},{8,9},{9,10},{10,1... | collective-permute-start | bytes 4616 | tf_op jit(solution)/shard_map/ppermute | solution.py:217
  50.8 0.0 collective-permute-start.10
  50.8 1.9 %collective-permute-start.9 = (f32[8,48]{1,0:T(8,128)S(1)}, f32[8,48]{1,0:T(8,128)S(1)}, u32[]{:S(2)}, u32[]{:S(2)}) collective-permute-start(f32[8,48]{1,0:T(8,128)S(1)} %bitcast.127), channel_id=1, source_target_pairs={{0,16},{16,32},{32,48},{48,64},{64,80},{80,96},{96,112},{112,128},... | collective-permute-start | bytes 4616 | tf_op jit(solution)/shard_map/ppermute | solution.py:217
  52.7 7.2 %collective-permute-start.8 = (f32[8,48]{1,0:T(8,128)S(1)}, f32[8,48]{1,0:T(8,128)S(1)}, u32[]{:S(2)}, u32[]{:S(2)}) collective-permute-start(f32[8,48]{1,0:T(8,128)S(1)} %bitcast.128), channel_id=1, source_target_pairs={{0,1008},{16,0},{32,16},{48,32},{64,48},{80,64},{96,80},{112,96},{... | collective-permute-start | bytes 4616 | tf_op jit(solution)/shard_map/ppermute | solution.py:217
  60.0 0.7 collective-permute-done.8
  60.7 0.0 collective-permute-done.10
  60.7 0.0 collective-permute-done.11
  60.7 0.7 fusion
  61.4 0.3 fusion.4
  61.7 0.1 copy.19
  61.8 0.0 copy-done.2
  61.9 1.3 %shard_map.88 = (f32[12,16,128]{2,1,0:T(8,128)}, f32[24,128]{1,0:T(8,128)S(1)}, f32[24,128]{1,0:T(8,128)S(1)}, f32[24,128]{1,0:T(8,128)S(1)}, f32[24,128]{1,0:T(8,128)S(1)}) custom-call(f32[12,16,128]{2,1,0:T(8,128)S(1)} %bitcast.108, bf16[36,16,128]{2,1,0:T(8,128)(2,1)S(1)} %bitcast.102, bf16[576,16,128]{2,1,0:T(8,128)(2,1)S(1)} %bitcast.99, ...), custom_call_target="tpu_custom_call" | custom-call | tf_op jit(solution)/shard_map/pallas_call | solution.py:205
  63.2 1.9 %collective-permute-start.12 = (f32[24,128]{1,0:T(8,128)S(1)}, f32[24,128]{1,0:T(8,128)S(1)}, u32[]{:S(2)}, u32[]{:S(2)}) collective-permute-start(f32[24,128]{1,0:T(8,128)S(1)} %get-tuple-element.16), channel_id=1, source_target_pairs={{0,16},{16,32},{32,48},{48,64},{64,80},{80,96},{96,112},{112,128},... | collective-permute-start | bytes 36872 | tf_op jit(solution)/shard_map/ppermute | solution.py:217
  65.1 7.0 %collective-permute-start.13 = (f32[24,128]{1,0:T(8,128)S(1)}, f32[24,128]{1,0:T(8,128)S(1)}, u32[]{:S(2)}, u32[]{:S(2)}) collective-permute-start(f32[24,128]{1,0:T(8,128)S(1)} %get-tuple-element.17), channel_id=1, source_target_pairs={{0,1008},{16,0},{32,16},{48,32},{64,48},{80,64},{96,80},{112,96},{... | collective-permute-start | bytes 36872 | tf_op jit(solution)/shard_map/ppermute | solution.py:217
  72.1 4.4 %collective-permute-start.14 = (f32[24,128]{1,0:T(8,128)S(1)}, f32[24,128]{1,0:T(8,128)S(1)}, u32[]{:S(2)}, u32[]{:S(2)}) collective-permute-start(f32[24,128]{1,0:T(8,128)S(1)} %get-tuple-element.18), channel_id=1, source_target_pairs={{0,1},{1,2},{2,3},{3,4},{4,5},{5,6},{6,7},{7,8},{8,9},{9,10},{10,1... | collective-permute-start | bytes 36872 | tf_op jit(solution)/shard_map/ppermute | solution.py:217
  76.4 0.0 collective-permute-done.13.t_ahead
  76.4 0.8 collective-permute-done.14.x_back
  77.3 3.5 %collective-permute-done.15.x_ahead = f32[24,128]{1,0:T(8,128)S(1)} collective-permute-done((f32[24,128]{1,0:T(8,128)S(1)}, f32[24,128]{1,0:T(8,128)S(1)}, u32[]{:S(2)}, u32[]{:S(2)}) %collective-permute-start.15) | collective-permute-done | bytes 12320 | tf_op jit(solution)/shard_map/ppermute | solution.py:217
  80.8 0.9 %copy-done.11 = f32[12,16,128]{2,1,0:T(8,128)S(1)} copy-done((f32[12,16,128]{2,1,0:T(8,128)S(1)}, f32[12,16,128]{2,1,0:T(8,128)}, u32[]{:S(2)}) %copy-start.11) | copy-done | bytes 98328
  81.7 0.9 %shard_map.89 = f32[12,16,128]{2,1,0:T(8,128)} custom-call(f32[12,16,128]{2,1,0:T(8,128)S(1)} %copy-done.11, f32[12,16,128]{2,1,0:T(8,128)S(1)} %bitcast.110, bf16[36,16,128]{2,1,0:T(8,128)(2,1)S(1)} %bitcast.103, bf16[72,16,128]{2,1,0:T(8,128)(2,1)S(1)} %bitcast.105, f32[24,128]{1,0:T(8,128)S(1)} %collective-permute-done.12.t_back, ...), custom_call_target="tpu_custom_call" | custom-call | tf_op jit(solution)/shard_map/pallas_call | solution.py:205
  (49 shorter events, 0.2 us)
Async XLA Ops:
  0.6 45.5 %copy-start = (bf16[8,1,1,8,48,48]{5,4,3,2,1,0:T(8,128)(2,1)S(1)}, bf16[8,1,1,8,48,48]{5,4,3,2,1,0:T(8,128)(2,1)}, u32[]{:S(2)}) copy-start(bf16[8,1,1,8,48,48]{5,4,3,2,1,0:T(8,128)(2,1)} %param.13) | copy-start | bytes 884740
  0.6 1.0 %copy-start.3 = (bf16[4,3,3,4,4,128]{5,4,3,2,1,0:T(4,128)(2,1)S(1)}, bf16[4,3,3,4,4,128]{5,4,3,2,1,0:T(4,128)(2,1)}, u32[]{:S(2)}) copy-start(bf16[4,3,3,4,4,128]{5,4,3,2,1,0:T(4,128)(2,1)} %param.9) | copy-start | bytes 442372
  1.6 0.9 %copy-start.7 = (f32[12,4,4,128]{3,2,1,0:T(4,128)S(1)}, f32[12,4,4,128]{3,2,1,0:T(4,128)}, u32[]{:S(2)}) copy-start(f32[12,4,4,128]{3,2,1,0:T(4,128)} %param.7) | copy-start | bytes 294916
  2.5 33.3 %copy-start.12 = (bf16[1,1,8,48,48]{4,3,2,1,0:T(8,128)(2,1)S(1)}, bf16[1,1,8,48,48]{4,3,2,1,0:T(8,128)(2,1)}, u32[]{:S(2)}) copy-start(bf16[1,1,8,48,48]{4,3,2,1,0:T(8,128)(2,1)} %param.12) | copy-start | bytes 110596
  2.6 24.8 %collective-permute-start = (f32[24,128]{1,0:T(8,128)S(1)}, f32[24,128]{1,0:T(8,128)S(1)}, u32[]{:S(2)}, u32[]{:S(2)}) collective-permute-start(f32[24,128]{1,0:T(8,128)S(1)} %get-tuple-element.11), channel_id=1, source_target_pairs={{0,16},{16,32},{32,48},{48,64},{64,80},{80,96},{96,112},{112,128},... | collective-permute-start | bytes 36872 | tf_op jit(solution)/shard_map/ppermute | solution.py:217
  7.5 19.8 %collective-permute-start.1 = (f32[24,128]{1,0:T(8,128)S(1)}, f32[24,128]{1,0:T(8,128)S(1)}, u32[]{:S(2)}, u32[]{:S(2)}) collective-permute-start(f32[24,128]{1,0:T(8,128)S(1)} %get-tuple-element.12), channel_id=1, source_target_pairs={{0,1008},{16,0},{32,16},{48,32},{64,48},{80,64},{96,80},{112,96},{... | collective-permute-start | bytes 36872 | tf_op jit(solution)/shard_map/ppermute | solution.py:217
  23.8 4.3 %collective-permute-start.2 = (f32[24,128]{1,0:T(8,128)S(1)}, f32[24,128]{1,0:T(8,128)S(1)}, u32[]{:S(2)}, u32[]{:S(2)}) collective-permute-start(f32[24,128]{1,0:T(8,128)S(1)} %get-tuple-element.13), channel_id=1, source_target_pairs={{0,1},{1,2},{2,3},{3,4},{4,5},{5,6},{6,7},{7,8},{8,9},{9,10},{10,1... | collective-permute-start | bytes 36872 | tf_op jit(solution)/shard_map/ppermute | solution.py:217
  27.3 4.3 %collective-permute-start.3 = (f32[24,128]{1,0:T(8,128)S(1)}, f32[24,128]{1,0:T(8,128)S(1)}, u32[]{:S(2)}, u32[]{:S(2)}) collective-permute-start(f32[24,128]{1,0:T(8,128)S(1)} %get-tuple-element.14), channel_id=1, source_target_pairs={{0,15},{1,0},{2,1},{3,2},{4,3},{5,4},{6,5},{7,6},{8,7},{9,8},{10,9... | collective-permute-start | bytes 36872 | tf_op jit(solution)/shard_map/ppermute | solution.py:217
  31.6 1.7 %copy-start.1 = (bf16[48,12,4,4,128]{4,3,2,1,0:T(4,128)(2,1)S(1)}, bf16[48,12,4,4,128]{4,3,2,1,0:T(4,128)(2,1)}, u32[]{:S(2)}) copy-start(bf16[48,12,4,4,128]{4,3,2,1,0:T(4,128)(2,1)} %param.11) | copy-start | bytes 7077892
  33.3 1.0 %copy-start.5 = (bf16[2,6,6,4,4,128]{5,4,3,2,1,0:T(4,128)(2,1)S(1)}, bf16[2,6,6,4,4,128]{5,4,3,2,1,0:T(4,128)(2,1)}, u32[]{:S(2)}) copy-start(bf16[2,6,6,4,4,128]{5,4,3,2,1,0:T(4,128)(2,1)} %param.10) | copy-start | bytes 884740
  34.3 0.9 %copy-start.9 = (f32[12,4,4,128]{3,2,1,0:T(4,128)S(1)}, f32[12,4,4,128]{3,2,1,0:T(4,128)}, u32[]{:S(2)}) copy-start(f32[12,4,4,128]{3,2,1,0:T(4,128)} %param.8) | copy-start | bytes 294916
  35.2 26.7 %copy-start.2 = (bf16[48,12,4,4,128]{4,3,2,1,0:T(4,128)(2,1)S(1)}, bf16[48,12,4,4,128]{4,3,2,1,0:T(4,128)(2,1)}, u32[]{:S(2)}) copy-start(bf16[48,12,4,4,128]{4,3,2,1,0:T(4,128)(2,1)} %param.11) | copy-start | bytes 7077892
  35.2 26.7 %copy-start.4 = (bf16[4,3,3,4,4,128]{5,4,3,2,1,0:T(4,128)(2,1)S(1)}, bf16[4,3,3,4,4,128]{5,4,3,2,1,0:T(4,128)(2,1)}, u32[]{:S(2)}) copy-start(bf16[4,3,3,4,4,128]{5,4,3,2,1,0:T(4,128)(2,1)} %param.9) | copy-start | bytes 442372
  35.2 26.7 %copy-start.8 = (f32[12,4,4,128]{3,2,1,0:T(4,128)S(1)}, f32[12,4,4,128]{3,2,1,0:T(4,128)}, u32[]{:S(2)}) copy-start(f32[12,4,4,128]{3,2,1,0:T(4,128)} %param.7) | copy-start | bytes 294916
  36.1 9.9 %collective-permute-start.7 = (f32[8,48]{1,0:T(8,128)S(1)}, f32[8,48]{1,0:T(8,128)S(1)}, u32[]{:S(2)}, u32[]{:S(2)}) collective-permute-start(f32[8,48]{1,0:T(8,128)S(1)} %bitcast.118), channel_id=1, source_target_pairs={{0,1},{1,2},{2,3},{3,4},{4,5},{5,6},{6,7},{7,8},{8,9},{9,10},{10,1... | collective-permute-start | bytes 4616 | tf_op jit(solution)/shard_map/ppermute | solution.py:217
  36.2 9.8 %collective-permute-start.6 = (f32[8,48]{1,0:T(8,128)S(1)}, f32[8,48]{1,0:T(8,128)S(1)}, u32[]{:S(2)}, u32[]{:S(2)}) collective-permute-start(f32[8,48]{1,0:T(8,128)S(1)} %bitcast.119), channel_id=1, source_target_pairs={{0,15},{1,0},{2,1},{3,2},{4,3},{5,4},{6,5},{7,6},{8,7},{9,8},{10,9... | collective-permute-start | bytes 4616 | tf_op jit(solution)/shard_map/ppermute | solution.py:217
  36.7 9.3 %collective-permute-start.5 = (f32[8,48]{1,0:T(8,128)S(1)}, f32[8,48]{1,0:T(8,128)S(1)}, u32[]{:S(2)}, u32[]{:S(2)}) collective-permute-start(f32[8,48]{1,0:T(8,128)S(1)} %bitcast.120), channel_id=1, source_target_pairs={{0,16},{16,32},{32,48},{48,64},{64,80},{80,96},{96,112},{112,128},... | collective-permute-start | bytes 4616 | tf_op jit(solution)/shard_map/ppermute | solution.py:217
  38.6 7.4 %collective-permute-start.4 = (f32[8,48]{1,0:T(8,128)S(1)}, f32[8,48]{1,0:T(8,128)S(1)}, u32[]{:S(2)}, u32[]{:S(2)}) collective-permute-start(f32[8,48]{1,0:T(8,128)S(1)} %bitcast.121), channel_id=1, source_target_pairs={{0,1008},{16,0},{32,16},{48,32},{64,48},{80,64},{96,80},{112,96},{... | collective-permute-start | bytes 4616 | tf_op jit(solution)/shard_map/ppermute | solution.py:217
  46.1 34.7 %copy-start.10 = (f32[12,4,4,128]{3,2,1,0:T(4,128)S(1)}, f32[12,4,4,128]{3,2,1,0:T(4,128)}, u32[]{:S(2)}) copy-start(f32[12,4,4,128]{3,2,1,0:T(4,128)} %param.8) | copy-start | bytes 294916
  47.1 13.5 %collective-permute-start.11 = (f32[8,48]{1,0:T(8,128)S(1)}, f32[8,48]{1,0:T(8,128)S(1)}, u32[]{:S(2)}, u32[]{:S(2)}) collective-permute-start(f32[8,48]{1,0:T(8,128)S(1)} %bitcast.125), channel_id=1, source_target_pairs={{0,1},{1,2},{2,3},{3,4},{4,5},{5,6},{6,7},{7,8},{8,9},{9,10},{10,1... | collective-permute-start | bytes 4616 | tf_op jit(solution)/shard_map/ppermute | solution.py:217
  50.8 9.9 %collective-permute-start.10 = (f32[8,48]{1,0:T(8,128)S(1)}, f32[8,48]{1,0:T(8,128)S(1)}, u32[]{:S(2)}, u32[]{:S(2)}) collective-permute-start(f32[8,48]{1,0:T(8,128)S(1)} %bitcast.126), channel_id=1, source_target_pairs={{0,15},{1,0},{2,1},{3,2},{4,3},{5,4},{6,5},{7,6},{8,7},{9,8},{10,9... | collective-permute-start | bytes 4616 | tf_op jit(solution)/shard_map/ppermute | solution.py:217
  50.8 9.9 %collective-permute-start.9 = (f32[8,48]{1,0:T(8,128)S(1)}, f32[8,48]{1,0:T(8,128)S(1)}, u32[]{:S(2)}, u32[]{:S(2)}) collective-permute-start(f32[8,48]{1,0:T(8,128)S(1)} %bitcast.127), channel_id=1, source_target_pairs={{0,16},{16,32},{32,48},{48,64},{64,80},{80,96},{96,112},{112,128},... | collective-permute-start | bytes 4616 | tf_op jit(solution)/shard_map/ppermute | solution.py:217
  52.7 8.0 %collective-permute-start.8 = (f32[8,48]{1,0:T(8,128)S(1)}, f32[8,48]{1,0:T(8,128)S(1)}, u32[]{:S(2)}, u32[]{:S(2)}) collective-permute-start(f32[8,48]{1,0:T(8,128)S(1)} %bitcast.128), channel_id=1, source_target_pairs={{0,1008},{16,0},{32,16},{48,32},{64,48},{80,64},{96,80},{112,96},{... | collective-permute-start | bytes 4616 | tf_op jit(solution)/shard_map/ppermute | solution.py:217
  61.8 19.0 %copy-start.6 = (bf16[2,6,6,4,4,128]{5,4,3,2,1,0:T(4,128)(2,1)S(1)}, bf16[2,6,6,4,4,128]{5,4,3,2,1,0:T(4,128)(2,1)}, u32[]{:S(2)}) copy-start(bf16[2,6,6,4,4,128]{5,4,3,2,1,0:T(4,128)(2,1)} %param.10) | copy-start | bytes 884740
  63.2 13.3 %collective-permute-start.12 = (f32[24,128]{1,0:T(8,128)S(1)}, f32[24,128]{1,0:T(8,128)S(1)}, u32[]{:S(2)}, u32[]{:S(2)}) collective-permute-start(f32[24,128]{1,0:T(8,128)S(1)} %get-tuple-element.16), channel_id=1, source_target_pairs={{0,16},{16,32},{32,48},{48,64},{64,80},{80,96},{96,112},{112,128},... | collective-permute-start | bytes 36872 | tf_op jit(solution)/shard_map/ppermute | solution.py:217
  65.1 11.3 %collective-permute-start.13 = (f32[24,128]{1,0:T(8,128)S(1)}, f32[24,128]{1,0:T(8,128)S(1)}, u32[]{:S(2)}, u32[]{:S(2)}) collective-permute-start(f32[24,128]{1,0:T(8,128)S(1)} %get-tuple-element.17), channel_id=1, source_target_pairs={{0,1008},{16,0},{32,16},{48,32},{64,48},{80,64},{96,80},{112,96},{... | collective-permute-start | bytes 36872 | tf_op jit(solution)/shard_map/ppermute | solution.py:217
  72.1 5.2 %collective-permute-start.14 = (f32[24,128]{1,0:T(8,128)S(1)}, f32[24,128]{1,0:T(8,128)S(1)}, u32[]{:S(2)}, u32[]{:S(2)}) collective-permute-start(f32[24,128]{1,0:T(8,128)S(1)} %get-tuple-element.18), channel_id=1, source_target_pairs={{0,1},{1,2},{2,3},{3,4},{4,5},{5,6},{6,7},{7,8},{8,9},{9,10},{10,1... | collective-permute-start | bytes 36872 | tf_op jit(solution)/shard_map/ppermute | solution.py:217
  76.4 4.3 %collective-permute-start.15 = (f32[24,128]{1,0:T(8,128)S(1)}, f32[24,128]{1,0:T(8,128)S(1)}, u32[]{:S(2)}, u32[]{:S(2)}) collective-permute-start(f32[24,128]{1,0:T(8,128)S(1)} %get-tuple-element.19), channel_id=1, source_target_pairs={{0,15},{1,0},{2,1},{3,2},{4,3},{5,4},{6,5},{7,6},{8,7},{9,8},{10,9... | collective-permute-start | bytes 36872 | tf_op jit(solution)/shard_map/ppermute | solution.py:217
  80.8 0.9 %copy-start.11 = (f32[12,16,128]{2,1,0:T(8,128)S(1)}, f32[12,16,128]{2,1,0:T(8,128)}, u32[]{:S(2)}) copy-start(f32[12,16,128]{2,1,0:T(8,128)} %get-tuple-element.15.field_ref) | copy-start | bytes 294916

commit v2 on v1

v2 whole, which is shorter than its diff:
```python
import jax
import jax.numpy as jnp
from jax import lax
from jax.experimental import pallas as pl
from jax.experimental.pallas import tpu as pltpu
from jax.sharding import PartitionSpec as P

CY = 8
CZ = 16
SWEEPS = 2
ROWS = 16
LANES = 128
FACE = 4
SPAN = 4

exact_mode = lax.Precision.HIGHEST
hopping = 0.5
wilson_mass = 4.0

VMEM = pl.BlockSpec(memory_space=pltpu.VMEM)
SMEM = pl.BlockSpec(memory_space=pltpu.SMEM)
HBM = pl.BlockSpec(memory_space=pltpu.HBM)
LIMIT = 24 * 1024 * 1024

EXPAND = {
    (0, 1): ((0, 0, 1), (1, 1, 1), (2, 0, -1), (3, 1, -1)),
    (0, -1): ((0, 0, 1), (1, 1, 1), (2, 0, 1), (3, 1, 1)),
    (1, 1): ((0, 0, 1), (3, 0, -1), (1, 1, 1), (2, 1, -1)),
    (1, -1): ((0, 0, 1), (3, 0, 1), (1, 1, 1), (2, 1, 1)),
    (2, 1): ((2, 0, 1), (3, 1, 1)),
    (2, -1): ((0, 0, 1), (1, 1, 1)),
    (3, 1): ((0, 0, 1), (1, 0, -1), (2, 1, 1), (3, 1, 1)),
    (3, -1): ((0, 0, 1), (1, 0, 1), (2, 1, 1), (3, 1, -1)),
}


def half(v, axis, direction):
    def mix(a, b, sign):
        return [v[a * 3 + c] + v[b * 3 + c] if sign > 0 else v[a * 3 + c] - v[b * 3 + c] for c in range(3)]

    if axis == 0:
        return mix(0, 2, -direction) + mix(1, 3, -direction)
    if axis == 1:
        return mix(0, 3, -direction) + mix(1, 2, -direction)
    if axis == 2:
        first = 2 if direction == 1 else 0
        return [2.0 * v[first * 3 + c] for c in range(6)]
    return mix(0, 1, -direction) + mix(2, 3, direction)


def transport(links_ref, axis, h, transposed):
    found = [None] * 6
    for i in range(3):
        for j in range(3):
            u = links_ref[axis * 9 + (j * 3 + i if transposed else i * 3 + j)].astype(jnp.float32)
            for spin in range(2):
                term = u * h[spin * 3 + j]
                at = spin * 3 + i
                found[at] = term if found[at] is None else found[at] + term
    return found


def place(dim):
    return lax.broadcasted_iota(jnp.int32, (ROWS, LANES), dim)


def edge_mask(axis, direction):
    rows = place(0)
    where = rows // FACE if axis == 0 else rows % FACE
    return where == (FACE - 1 if direction == 1 else 0)


def shifted(value, axis, direction):
    if axis < 2:
        moved = pltpu.roll(value, (-direction * (FACE if axis == 0 else 1)) % ROWS, 0)
        return jnp.where(edge_mask(axis, direction), 0.0, moved)
    if axis == 2:
        return pltpu.roll(value, (-direction * CZ) % LANES, 1)
    inside = pltpu.roll(value, (-direction) % LANES, 1)
    wrapped = pltpu.roll(value, (direction * (CZ - 1)) % LANES, 1)
    edge = CZ - 1 if direction == 1 else 0
    return jnp.where(place(1) % CZ == edge, wrapped, inside)


def halo_tile(face, axis, direction):
    if axis == 0:
        tile = jnp.concatenate([face] * (ROWS // FACE), axis=0)
    else:
        tile = jnp.broadcast_to(face[0:1], (ROWS, LANES))
        for t in range(1, FACE):
            tile = jnp.where(place(0) // FACE == t, jnp.broadcast_to(face[t : t + 1], (ROWS, LANES)), tile)
    return jnp.where(edge_mask(axis, direction), tile, 0.0)


def add_hop(hops, near, axis, direction):
    for spin, part, sign in EXPAND[axis, direction]:
        for c in range(3):
            at, term = spin * 3 + c, near[part * 3 + c]
            if hops[at] is None:
                hops[at] = term if sign > 0 else -term
            else:
                hops[at] = hops[at] + term if sign > 0 else hops[at] - term


def dirac_inside(v, links_ref, clover_ref):
    hops = [None] * 12
    for axis in range(4):
        for direction in (1, -1):
            h = half(v, axis, direction)
            if direction == -1:
                h = transport(links_ref, axis, h, True)
            near = []
            for c in range(6):
                near.append(shifted(h[c], axis, direction))
            if direction == 1:
                near = transport(links_ref, axis, near, False)
            add_hop(hops, near, axis, direction)
    total = []
    for block in range(2):
        for i in range(6):
            local = None
            for j in range(6):
                term = clover_ref[(block * 6 + i) * 6 + j].astype(jnp.float32) * v[block * 6 + j]
                local = term if local is None else local + term
            at = block * 6 + i
            total.append(wilson_mass * v[at] + local - hopping * hops[at])
    return total


def rows_of(c):
    return slice(c * FACE, (c + 1) * FACE)


def write_faces(v, links_ref, odd, faces, work_ref):
    t_first, t_second, x_up, x_down = faces
    back = transport(links_ref, 0, half(v, 0, -1), True)
    ahead = half(v, 0, 1)
    for c in range(6):
        up, down = back[c][ROWS - FACE :], ahead[c][:FACE]
        t_first[rows_of(c), :] = jnp.where(odd, down, up)
        t_second[rows_of(c), :] = jnp.where(odd, up, down)
    back = transport(links_ref, 1, half(v, 1, -1), True)
    ahead = half(v, 1, 1)
    for c in range(6):
        work_ref[c] = back[c]
        work_ref[6 + c] = ahead[c]
    for c in range(6):
        x_up[rows_of(c), :] = work_ref[c, pl.ds(FACE - 1, FACE, stride=FACE), :]
        x_down[rows_of(c), :] = work_ref[6 + c, pl.ds(0, FACE, stride=FACE), :]


def faces_kernel(odd_ref, field_hbm, links_hbm, field_ref, links_ref, t_first, t_second, x_up, x_down, work_ref, sems):
    copies = [
        pltpu.make_async_copy(field_hbm, field_ref, sems.at[0]),
        pltpu.make_async_copy(links_hbm, links_ref, sems.at[1]),
    ]
    for copy in copies:
        copy.start()
    for copy in copies:
        copy.wait()
    field = [field_ref[m] for m in range(12)]
    write_faces(field, links_ref, odd_ref[0] == 1, (t_first, t_second, x_up, x_down), work_ref)


def inside_first_kernel(
    field_ref, links_ref, right_hbm, clover_hbm, null_hbm, inside_ref, right_ref, clover_ref, null_ref, sems
):
    copies = [
        pltpu.make_async_copy(clover_hbm, clover_ref, sems.at[0]),
        pltpu.make_async_copy(right_hbm, right_ref, sems.at[1]),
        pltpu.make_async_copy(null_hbm, null_ref, sems.at[2]),
    ]
    for copy in copies:
        copy.start()
    copies[0].wait()
    copies[1].wait()
    total = dirac_inside([field_ref[m] for m in range(12)], links_ref, clover_ref)
    for m in range(12):
        inside_ref[m] = right_ref[m] - total[m]
    copies[2].wait()


def inside_kernel(field_ref, links_ref, right_ref, clover_ref, inside_ref, out_ref):
    field = [field_ref[m] for m in range(12)]
    total = dirac_inside(field, links_ref, clover_ref)
    for m in range(12):
        out_ref[m] = field[m]
        inside_ref[m] = right_ref[m] - total[m]


def residual_tiles(odd_ref, inside_ref, links_ref, x_back, x_ahead, t_first, t_second):
    odd = odd_ref[0] == 1
    hops = [None] * 12
    for axis in range(2):
        for direction in (1, -1):
            near = []
            for c in range(6):
                if axis == 1:
                    face = (x_ahead if direction == 1 else x_back)[rows_of(c), :]
                else:
                    first, second = t_first[rows_of(c), :], t_second[rows_of(c), :]
                    face = jnp.where(odd, second, first) if direction == 1 else jnp.where(odd, first, second)
                near.append(halo_tile(face, axis, direction))
            if direction == 1:
                near = transport(links_ref, axis, near, False)
            add_hop(hops, near, axis, direction)
    return [inside_ref[m] + hopping * hops[m] for m in range(12)]


def owner_table(blocks):
    places = lax.broadcasted_iota(jnp.int32, (blocks, LANES), 1)
    owners = places // (CZ * SPAN) * (CZ // SPAN) + places % CZ // SPAN
    return owners == lax.broadcasted_iota(jnp.int32, (blocks, LANES), 0)


def pieces(value, count):
    found = []
    for _ in range(count):
        part = value.astype(jnp.bfloat16)
        value = value - part.astype(jnp.float32)
        found.append(part)
    return found


def times_inverse(value, inverse_ref):
    blocks = value.shape[0]
    parts = pieces(value, 3)
    rows = []
    for s in range(blocks):
        total = None
        for part in parts:
            term = lax.dot_general(part, inverse_ref[s], (((1,), (1,)), ((), ())), preferred_element_type=jnp.float32)
            total = term if total is None else total + term
        rows.append(total[s : s + 1])
    return jnp.concatenate(rows, axis=0)


def sweep(odd, approx_ref, rhs_ref, near_refs, couplings_ref, inverse_ref):
    x_back, x_ahead, t_first, t_second = near_refs
    blocks, channels = approx_ref.shape
    first, second = t_first[...], t_second[...]
    ahead, back = jnp.where(odd, second, first), jnp.where(odd, first, second)
    mine, right, left = approx_ref[...], x_ahead[...], x_back[...]
    ones = jnp.ones((blocks, channels), jnp.bfloat16)
    deep = CZ // SPAN
    rows = []
    for s in range(blocks):
        other, z = (s + deep) % blocks, s // deep * deep
        up, down = z + (s + 1) % deep, z + (s - 1) % deep
        sources = (ahead, s), (back, s), (right, s), (left, s), (mine, other), (mine, other), (mine, up), (mine, down)
        total = None
        for d, (source, at) in enumerate(sources):
            row = jnp.broadcast_to(source[at : at + 1], (channels, channels))
            term = couplings_ref[d * blocks + s].astype(jnp.float32) * row
            total = term if total is None else total + term
        off = None
        for part in pieces(total, 2):
            term = lax.dot_general(ones, part, (((1,), (1,)), ((), ())), preferred_element_type=jnp.float32)
            off = term if off is None else off + term
        rows.append(off[s : s + 1])
    return times_inverse(rhs_ref[...] - jnp.concatenate(rows, axis=0), inverse_ref)


def sweep_kernel(
    odd_ref, approx_ref, rhs_ref, x_back, x_ahead, t_first, t_second, couplings_ref, inverse_ref, out_ref
):
    near = (x_back, x_ahead, t_first, t_second)
    out_ref[...] = sweep(odd_ref[0] == 1, approx_ref, rhs_ref, near, couplings_ref, inverse_ref)


def restrict_kernel(
    odd_ref, inside_ref, links_ref, x_back, x_ahead, t_first, t_second, null_ref, inverse_ref, coarse_ref, approx_ref, summed_ref
):
    residual = residual_tiles(odd_ref, inside_ref, links_ref, x_back, x_ahead, t_first, t_second)
    rough = [r.astype(jnp.bfloat16).astype(jnp.float32) for r in residual]
    channels = summed_ref.shape[0]

    def one(k, _):
        total = None
        for m in range(12):
            term = null_ref[k * 12 + m].astype(jnp.float32) * rough[m]
            total = term if total is None else total + term
        summed_ref[pl.ds(k, 1), :] = jnp.sum(total, axis=0, keepdims=True)
        return 0

    lax.fori_loop(0, channels, one, 0, unroll=4)
    table = owner_table(coarse_ref.shape[0]).astype(jnp.float32)
    coarse = lax.dot_general(
        table, summed_ref[...], (((1,), (1,)), ((), ())), precision=exact_mode, preferred_element_type=jnp.float32
    )
    coarse_ref[...] = coarse
    approx_ref[...] = times_inverse(coarse, inverse_ref)


def prolong_kernel(
    odd_ref,
    approx_ref,
    rhs_ref,
    x_back,
    x_ahead,
    t_back,
    t_ahead,
    couplings_ref,
    inverse_ref,
    field_ref,
    links_ref,
    null_ref,
    updated_ref,
    t_first,
    t_second,
    x_up,
    x_down,
    spread_ref,
    work_ref,
):
    blocks, channels = approx_ref.shape
    near = (x_back, x_ahead, t_back, t_ahead)
    approx = sweep(odd_ref[0] == 1, approx_ref, rhs_ref, near, couplings_ref, inverse_ref)
    table = owner_table(blocks).astype(jnp.bfloat16)
    spread_ref[...] = lax.dot_general(
        approx.astype(jnp.bfloat16), table, (((0,), (0,)), ((), ())), preferred_element_type=jnp.float32
    )

    def one(k, totals):
        row = jnp.broadcast_to(spread_ref[pl.ds(k, 1), :], (ROWS, LANES))
        return tuple(totals[m] + null_ref[k * 12 + m].astype(jnp.float32) * row for m in range(12))

    start = tuple(jnp.zeros((ROWS, LANES), jnp.float32) for _ in range(12))
    added = lax.fori_loop(0, channels, one, start, unroll=4)
    updated = [field_ref[m] + added[m] for m in range(12)]
    for m in range(12):
        updated_ref[m] = updated[m]
    write_faces(updated, links_ref, odd_ref[0] == 1, (t_first, t_second, x_up, x_down), work_ref)


def residual_kernel(odd_ref, inside_ref, links_ref, x_back, x_ahead, t_first, t_second, out_ref):
    residual = residual_tiles(odd_ref, inside_ref, links_ref, x_back, x_ahead, t_first, t_second)
    for m in range(12):
        out_ref[m] = residual[m]


def call(kernel, outs, scratch, *args, far=(), sems=0, cost=None):
    args = [pltpu.with_memory_space_constraint(arg, pltpu.HBM) if i in far else arg for i, arg in enumerate(args)]
    scratch_shapes = [pltpu.VMEM(shape, jnp.float32) for shape in scratch]
    if sems:
        scratch_shapes.append(pltpu.SemaphoreType.DMA((sems,)))
    return pl.pallas_call(
        kernel,
        out_shape=[jax.ShapeDtypeStruct(*out) for out in outs],
        in_specs=[SMEM if arg.dtype == jnp.int32 else HBM if i in far else VMEM for i, arg in enumerate(args)],
        out_specs=[VMEM] * len(outs),
        scratch_shapes=scratch_shapes,
        compiler_params=pltpu.CompilerParams(vmem_limit_bytes=LIMIT),
        cost_estimate=cost,
    )(*args)


def moved(value, axis, step):
    size = lax.axis_size(axis)
    return lax.ppermute(value, axis, [(i, (i + step) % size) for i in range(size)])


def traded(value, axis, second):
    size = lax.axis_size(axis)
    return lax.ppermute(value, axis, [(i, (i + (1 if i % 2 == second else -1)) % size) for i in range(size)])


def swapped(x_up, x_down, t_first, t_second):
    return moved(x_up, "agg", 1), moved(x_down, "agg", -1), traded(t_first, "lat", 0), traded(t_second, "lat", 1)


def shards(solution, right_side, links, clover, null_vectors, coarse_inverse, coarse_links):
    shape = solution.shape
    blocks, channels = coarse_inverse.shape[2], coarse_inverse.shape[-1]
    field = solution.reshape(12, ROWS, LANES)
    right = right_side.reshape(field.shape)
    link_tiles = links.reshape(36, ROWS, LANES)
    clover_tiles = clover.reshape(72, ROWS, LANES)
    null_tiles = null_vectors.reshape(channels * 12, ROWS, LANES)
    inverse = coarse_inverse.reshape(blocks, channels, channels)
    couplings = coarse_links.reshape(8 * blocks, channels, channels)

    tiles, face = (field.shape, jnp.float32), ((6 * FACE, LANES), jnp.float32)
    coarse = ((blocks, channels), jnp.float32)
    work, sums = field.shape, (channels, LANES)
    odd = (lax.axis_index("lat") % 2).astype(jnp.int32).reshape(1)
    beside = pl.CostEstimate(flops=4_000_000, bytes_accessed=6_000_000, transcendentals=0)

    def staged(array):
        return (array.shape, array.dtype)

    field, link_tiles, t_first, t_second, x_up, x_down = call(
        faces_kernel,
        [tiles, staged(link_tiles)] + [face] * 4,
        [work],
        odd,
        field,
        link_tiles,
        far=(1, 2),
        sems=2,
    )
    halos = swapped(x_up, x_down, t_first, t_second)
    inside, right, clover_tiles, null_tiles = call(
        inside_first_kernel,
        [tiles, tiles, staged(clover_tiles), staged(null_tiles)],
        [],
        field,
        link_tiles,
        right,
        clover_tiles,
        null_tiles,
        far=(2, 3, 4),
        sems=3,
        cost=beside,
    )
    rhs, approx = call(
        restrict_kernel, [coarse, coarse], [sums], odd, inside, link_tiles, *halos, null_tiles, inverse
    )
    for _ in range(SWEEPS - 1):
        near = swapped(approx, approx, approx, approx)
        (approx,) = call(sweep_kernel, [coarse], [], odd, approx, rhs, *near, couplings, inverse)
    near = swapped(approx, approx, approx, approx)
    updated, t_first, t_second, x_up, x_down = call(
        prolong_kernel,
        [tiles] + [face] * 4,
        [sums, work],
        odd,
        approx,
        rhs,
        *near,
        couplings,
        inverse,
        field,
        link_tiles,
        null_tiles,
    )
    halos = swapped(x_up, x_down, t_first, t_second)
    inside, updated = call(inside_kernel, [tiles, tiles], [], updated, link_tiles, right, clover_tiles, cost=beside)
    (after,) = call(residual_kernel, [tiles], [], odd, inside, link_tiles, *halos)
    return updated.reshape(shape), after.reshape(shape)


def solution(mesh):
    placed = (
        P(None, "lat", "agg", None),
        P(None, "lat", "agg", None),
        P(None, None, None, "lat", "agg", None),
        P(None, None, None, "lat", "agg", None),
        P(None, None, "lat", "agg", None),
        P("lat", "agg", None, None, None),
        P(None, "lat", "agg", None, None, None),
    )
    return jax.shard_map(
        shards,
        mesh=mesh,
        in_specs=placed,
        out_specs=(P(None, "lat", "agg", None), P(None, "lat", "agg", None)),
        check_vma=False,
    )
```

time: 83.1 us -> 69.8 us (0.84)
  the two profiles are of different devices: /device:TPU:49 before, /device:TPU:64 now
where the time goes in v2:
time: 69.8 us; the launch traced here: 69.4 us
  starting transfers between devices  52.3 us (75%)
  waiting for transfers between devices  9.16 us (13%)
  Pallas kernels  7.11 us (10%)
  between operations  0.82 us (1%)
    ppermute x8, starting transfers between devices, traded(): lax.ppermute(value, axis, [(i, (i + (1 if i % 2 == second else -1)) % siz...  45.4 us
    ppermute x8, waiting for transfers between devices, traded(): lax.ppermute(value, axis, [(i, (i + (1 if i % 2 == second else -1)) % siz...  7.12 us
    pallas_call x7, Pallas kernels, call(): pl.pallas_call(kernel, out_shape=[jax.ShapeDtypeStruct(*out) for out in o...  7.11 us
    ppermute x8, starting transfers between devices, moved(): lax.ppermute(value, axis, [(i, (i + step) % size) for i in range(size)])  6.95 us
    ppermute x8, waiting for transfers between devices, moved(): lax.ppermute(value, axis, [(i, (i + step) % size) for i in range(size)])  2.03 us
  transfers between devices with their start and end apart: 16, of which 5 were waited for; matrix products, arithmetic and copies ran while one was open for 0% of the time, Pallas kernels for 4%

profile of v2, /device:TPU:64, one launch (start us, length us, event | category | flops | bytes accessed | tf_op | source)
XLA Modules:
  0.0 69.4 jit_solution(736108224675105309)
XLA Ops:
  0.6 0.0 copy-start.1
  0.7 1.0 %shard_map.86 = (f32[12,16,128]{2,1,0:T(8,128)S(1)}, bf16[36,16,128]{2,1,0:T(8,128)(2,1)S(1)}, f32[24,128]{1,0:T(8,128)S(1)}, f32[24,128]{1,0:T(8,128)S(1)}, f32...) custom-call(s32[1]{0:T(128)} %bitcast.odd_ref, f32[12,16,128]{2,1,0:T(8,128)} %bitcast.19, bf16[36,16,128]{2,1,0:T(8,128)(2,1)} %bitcast.17), custom_call_target="tpu_custom_call" | custom-call | tf_op jit(solution)/shard_map/pallas_call | solution.py:347
  1.7 0.0 collective-permute-start
  1.7 2.9 %collective-permute-start.1 = (f32[24,128]{1,0:T(8,128)S(1)}, f32[24,128]{1,0:T(8,128)S(1)}, u32[]{:S(2)}, u32[]{:S(2)}) collective-permute-start(f32[24,128]{1,0:T(8,128)S(1)} %get-tuple-element.25), channel_id=1, source_target_pairs={{0,15},{1,0},{2,1},{3,2},{4,3},{5,4},{6,5},{7,6},{8,7},{9,8},{10,9... | collective-permute-start | bytes 36872 | tf_op jit(solution)/shard_map/ppermute | solution.py:360
  4.7 5.2 %collective-permute-start.2 = (f32[24,128]{1,0:T(8,128)S(1)}, f32[24,128]{1,0:T(8,128)S(1)}, u32[]{:S(2)}, u32[]{:S(2)}) collective-permute-start(f32[24,128]{1,0:T(8,128)S(1)} %get-tuple-element.26), channel_id=1, source_target_pairs={{0,16},{16,0},{32,48},{48,32},{64,80},{80,64},{96,112},{112,96},{1... | collective-permute-start | bytes 36872 | tf_op jit(solution)/shard_map/ppermute | solution.py:365
  9.9 16.4 %collective-permute-start.3 = (f32[24,128]{1,0:T(8,128)S(1)}, f32[24,128]{1,0:T(8,128)S(1)}, u32[]{:S(2)}, u32[]{:S(2)}) collective-permute-start(f32[24,128]{1,0:T(8,128)S(1)} %get-tuple-element.27), channel_id=1, source_target_pairs={{0,1008},{16,32},{32,16},{48,64},{64,48},{80,96},{96,80},{112,128}... | collective-permute-start | bytes 36872 | tf_op jit(solution)/shard_map/ppermute | solution.py:365
  26.2 0.0 copy-start
  26.2 1.9 %shard_map.87 = (f32[12,16,128]{2,1,0:T(8,128)S(1)}, f32[12,16,128]{2,1,0:T(8,128)S(1)}, bf16[72,16,128]{2,1,0:T(8,128)(2,1)S(1)}, bf16[576,16,128]{2,1,0:T(8,128)(2,1)S(1)}) custom-call(f32[12,16,128]{2,1,0:T(8,128)S(1)} %get-tuple-element.21.field_ref, bf16[36,16,128]{2,1,0:T(8,128)(2,1)S(1)} %get-tuple-element.22.links_ref, f32[12,16,128]{2,1,0:T(8,128)} %bitcast.18, ...), custom_call_target="tpu_custom_call" | custom-call | flops 4000000 | bytes 6000000 | tf_op jit(solution)/shard_map/pallas_call | solution.py:347
  28.1 0.0 collective-permute-done.x_back
  28.2 0.0 collective-permute-done.1.x_ahead
  28.2 0.0 collective-permute-done.2.t_first
  28.2 0.0 collective-permute-done.3.t_second
  28.2 0.0 copy-done.1
  28.2 0.8 %shard_map.88 = (f32[8,48]{1,0:T(8,128)S(1)}, f32[8,48]{1,0:T(8,128)S(1)}) custom-call(s32[1]{0:T(128)} %bitcast.odd_ref, f32[12,16,128]{2,1,0:T(8,128)S(1)} %get-tuple-element.23.inside_ref, bf16[36,16,128]{2,1,0:T(8,128)(2,1)S(1)} %get-tuple-element.22.links_ref, f32[24,128]{1,0:T(8,128)S(1)} %collective-permute-done.x_back, ...), custom_call_target="tpu_custom_call" | custom-call | tf_op jit(solution)/shard_map/pallas_call | solution.py:347
  29.0 6.9 %collective-permute-start.7 = (f32[8,48]{1,0:T(8,128)S(1)}, f32[8,48]{1,0:T(8,128)S(1)}, u32[]{:S(2)}, u32[]{:S(2)}) collective-permute-start(f32[8,48]{1,0:T(8,128)S(1)} %get-tuple-element.29.approx_ref), channel_id=1, source_target_pairs={{0,1008},{16,32},{32,16},{48,64},{64,48},{80,96},{96,80},{112,128}... | collective-permute-start | bytes 4616 | tf_op jit(solution)/shard_map/ppermute | solution.py:365
  36.0 1.9 %collective-permute-start.6 = (f32[8,48]{1,0:T(8,128)S(1)}, f32[8,48]{1,0:T(8,128)S(1)}, u32[]{:S(2)}, u32[]{:S(2)}) collective-permute-start(f32[8,48]{1,0:T(8,128)S(1)} %get-tuple-element.29.approx_ref), channel_id=1, source_target_pairs={{0,16},{16,0},{32,48},{48,32},{64,80},{80,64},{96,112},{112,96},{1... | collective-permute-start | bytes 4616 | tf_op jit(solution)/shard_map/ppermute | solution.py:365
  37.9 0.0 collective-permute-start.5
  37.9 0.5 collective-permute-start.4
  38.4 0.0 collective-permute-done.7.t_second
  38.4 3.0 %collective-permute-done.6.t_first = f32[8,48]{1,0:T(8,128)S(1)} collective-permute-done((f32[8,48]{1,0:T(8,128)S(1)}, f32[8,48]{1,0:T(8,128)S(1)}, u32[]{:S(2)}, u32[]{:S(2)}) %collective-permute-start.6) | collective-permute-done | bytes 1568 | tf_op jit(solution)/shard_map/ppermute | solution.py:365
  41.5 0.0 collective-permute-done.5.x_ahead
  41.5 0.7 %collective-permute-done.4.x_back = f32[8,48]{1,0:T(8,128)S(1)} collective-permute-done((f32[8,48]{1,0:T(8,128)S(1)}, f32[8,48]{1,0:T(8,128)S(1)}, u32[]{:S(2)}, u32[]{:S(2)}) %collective-permute-start.4) | collective-permute-done | bytes 1568 | tf_op jit(solution)/shard_map/ppermute | solution.py:360
  42.2 0.0 copy-done
  42.2 0.6 shard_map.89.approx_ref
  42.7 2.6 %collective-permute-start.11 = (f32[8,48]{1,0:T(8,128)S(1)}, f32[8,48]{1,0:T(8,128)S(1)}, u32[]{:S(2)}, u32[]{:S(2)}) collective-permute-start(f32[8,48]{1,0:T(8,128)S(1)} %shard_map.89.approx_ref), channel_id=1, source_target_pairs={{0,1008},{16,32},{32,16},{48,64},{64,48},{80,96},{96,80},{112,128}... | collective-permute-start | bytes 4616 | tf_op jit(solution)/shard_map/ppermute | solution.py:365
  45.4 3.2 %collective-permute-start.10 = (f32[8,48]{1,0:T(8,128)S(1)}, f32[8,48]{1,0:T(8,128)S(1)}, u32[]{:S(2)}, u32[]{:S(2)}) collective-permute-start(f32[8,48]{1,0:T(8,128)S(1)} %shard_map.89.approx_ref), channel_id=1, source_target_pairs={{0,16},{16,0},{32,48},{48,32},{64,80},{80,64},{96,112},{112,96},{1... | collective-permute-start | bytes 4616 | tf_op jit(solution)/shard_map/ppermute | solution.py:365
  48.6 0.0 collective-permute-start.9
  48.6 0.5 collective-permute-start.8
  49.1 2.4 %collective-permute-done.11.t_ahead = f32[8,48]{1,0:T(8,128)S(1)} collective-permute-done((f32[8,48]{1,0:T(8,128)S(1)}, f32[8,48]{1,0:T(8,128)S(1)}, u32[]{:S(2)}, u32[]{:S(2)}) %collective-permute-start.11) | collective-permute-done | bytes 1568 | tf_op jit(solution)/shard_map/ppermute | solution.py:365
  51.6 0.0 collective-permute-done.10.t_back
  51.6 0.0 collective-permute-done.9.x_ahead
  51.6 1.3 %collective-permute-done.8.x_back = f32[8,48]{1,0:T(8,128)S(1)} collective-permute-done((f32[8,48]{1,0:T(8,128)S(1)}, f32[8,48]{1,0:T(8,128)S(1)}, u32[]{:S(2)}, u32[]{:S(2)}) %collective-permute-start.8) | collective-permute-done | bytes 1568 | tf_op jit(solution)/shard_map/ppermute | solution.py:360
  52.9 1.3 %shard_map.90 = (f32[12,16,128]{2,1,0:T(8,128)S(1)}, f32[24,128]{1,0:T(8,128)S(1)}, f32[24,128]{1,0:T(8,128)S(1)}, f32[24,128]{1,0:T(8,128)S(1)}, f32[24,128]{1,0:T(8,128)S(1)}) custom-call(s32[1]{0:T(128)} %bitcast.odd_ref, f32[8,48]{1,0:T(8,128)S(1)} %shard_map.89.approx_ref, f32[8,48]{1,0:T(8,128)S(1)} %get-tuple-element.30.rhs_ref, ...), custom_call_target="tpu_custom_call" | custom-call | tf_op jit(solution)/shard_map/pallas_call | solution.py:347
  54.2 0.0 collective-permute-start.12
  54.3 2.9 %collective-permute-start.13 = (f32[24,128]{1,0:T(8,128)S(1)}, f32[24,128]{1,0:T(8,128)S(1)}, u32[]{:S(2)}, u32[]{:S(2)}) collective-permute-start(f32[24,128]{1,0:T(8,128)S(1)} %get-tuple-element.37), channel_id=1, source_target_pairs={{0,15},{1,0},{2,1},{3,2},{4,3},{5,4},{6,5},{7,6},{8,7},{9,8},{10,9... | collective-permute-start | bytes 36872 | tf_op jit(solution)/shard_map/ppermute | solution.py:360
  57.2 2.6 %collective-permute-start.14 = (f32[24,128]{1,0:T(8,128)S(1)}, f32[24,128]{1,0:T(8,128)S(1)}, u32[]{:S(2)}, u32[]{:S(2)}) collective-permute-start(f32[24,128]{1,0:T(8,128)S(1)} %get-tuple-element.38), channel_id=1, source_target_pairs={{0,16},{16,0},{32,48},{48,32},{64,80},{80,64},{96,112},{112,96},{1... | collective-permute-start | bytes 36872 | tf_op jit(solution)/shard_map/ppermute | solution.py:365
  59.8 6.5 %collective-permute-start.15 = (f32[24,128]{1,0:T(8,128)S(1)}, f32[24,128]{1,0:T(8,128)S(1)}, u32[]{:S(2)}, u32[]{:S(2)}) collective-permute-start(f32[24,128]{1,0:T(8,128)S(1)} %get-tuple-element.39), channel_id=1, source_target_pairs={{0,1008},{16,32},{32,16},{48,64},{64,48},{80,96},{96,80},{112,128}... | collective-permute-start | bytes 36872 | tf_op jit(solution)/shard_map/ppermute | solution.py:365
  66.4 0.7 %shard_map.91 = (f32[12,16,128]{2,1,0:T(8,128)S(1)}, f32[12,16,128]{2,1,0:T(8,128)}) custom-call(f32[12,16,128]{2,1,0:T(8,128)S(1)} %get-tuple-element.31.field_ref, bf16[36,16,128]{2,1,0:T(8,128)(2,1)S(1)} %get-tuple-element.22.links_ref, f32[12,16,128]{2,1,0:T(8,128)S(1)} %get-tuple-element.32.right_ref, bf16[72,16,128]{2,1,0:T(8,128)(2,1)S(1)} %get-tuple-element.33.clover_ref), custom_call_target="tpu_custom_call" | custom-call | flops 4000000 | bytes 6000000 | tf_op jit(solution)/shard_map/pallas_call | solution.py:347
  67.1 0.0 collective-permute-done.12.x_back
  67.1 0.0 collective-permute-done.13.x_ahead
  67.1 0.0 collective-permute-done.14.t_first
  67.1 1.6 %collective-permute-done.15.t_second = f32[24,128]{1,0:T(8,128)S(1)} collective-permute-done((f32[24,128]{1,0:T(8,128)S(1)}, f32[24,128]{1,0:T(8,128)S(1)}, u32[]{:S(2)}, u32[]{:S(2)}) %collective-permute-start.15) | collective-permute-done | bytes 12320 | tf_op jit(solution)/shard_map/ppermute | solution.py:365
  68.7 0.7 %shard_map.92 = f32[12,16,128]{2,1,0:T(8,128)} custom-call(s32[1]{0:T(128)} %bitcast.odd_ref, f32[12,16,128]{2,1,0:T(8,128)S(1)} %get-tuple-element.35.inside_ref, bf16[36,16,128]{2,1,0:T(8,128)(2,1)S(1)} %get-tuple-element.22.links_ref, f32[24,128]{1,0:T(8,128)S(1)} %collective-permute-done.12.x_back, f32[24,128]{1,0:T(8,128)S(1)} %collective-permute-done.13.x_ahead, ...), custom_call_target="tpu_custom_call" | custom-call | tf_op jit(solution)/shard_map/pallas_call | solution.py:347
Async XLA Ops:
  0.6 27.6 %copy-start.1 = (bf16[1,1,8,48,48]{4,3,2,1,0:T(8,128)(2,1)S(1)}, bf16[1,1,8,48,48]{4,3,2,1,0:T(8,128)(2,1)}, u32[]{:S(2)}) copy-start(bf16[1,1,8,48,48]{4,3,2,1,0:T(8,128)(2,1)} %param.12) | copy-start | bytes 110596
  1.7 26.4 %collective-permute-start = (f32[24,128]{1,0:T(8,128)S(1)}, f32[24,128]{1,0:T(8,128)S(1)}, u32[]{:S(2)}, u32[]{:S(2)}) collective-permute-start(f32[24,128]{1,0:T(8,128)S(1)} %get-tuple-element.24), channel_id=1, source_target_pairs={{0,1},{1,2},{2,3},{3,4},{4,5},{5,6},{6,7},{7,8},{8,9},{9,10},{10,1... | collective-permute-start | bytes 36872 | tf_op jit(solution)/shard_map/ppermute | solution.py:360
  1.7 26.4 %collective-permute-start.1 = (f32[24,128]{1,0:T(8,128)S(1)}, f32[24,128]{1,0:T(8,128)S(1)}, u32[]{:S(2)}, u32[]{:S(2)}) collective-permute-start(f32[24,128]{1,0:T(8,128)S(1)} %get-tuple-element.25), channel_id=1, source_target_pairs={{0,15},{1,0},{2,1},{3,2},{4,3},{5,4},{6,5},{7,6},{8,7},{9,8},{10,9... | collective-permute-start | bytes 36872 | tf_op jit(solution)/shard_map/ppermute | solution.py:360
  4.7 23.5 %collective-permute-start.2 = (f32[24,128]{1,0:T(8,128)S(1)}, f32[24,128]{1,0:T(8,128)S(1)}, u32[]{:S(2)}, u32[]{:S(2)}) collective-permute-start(f32[24,128]{1,0:T(8,128)S(1)} %get-tuple-element.26), channel_id=1, source_target_pairs={{0,16},{16,0},{32,48},{48,32},{64,80},{80,64},{96,112},{112,96},{1... | collective-permute-start | bytes 36872 | tf_op jit(solution)/shard_map/ppermute | solution.py:365
  9.9 18.3 %collective-permute-start.3 = (f32[24,128]{1,0:T(8,128)S(1)}, f32[24,128]{1,0:T(8,128)S(1)}, u32[]{:S(2)}, u32[]{:S(2)}) collective-permute-start(f32[24,128]{1,0:T(8,128)S(1)} %get-tuple-element.27), channel_id=1, source_target_pairs={{0,1008},{16,32},{32,16},{48,64},{64,48},{80,96},{96,80},{112,128}... | collective-permute-start | bytes 36872 | tf_op jit(solution)/shard_map/ppermute | solution.py:365
  26.2 16.0 %copy-start = (bf16[8,1,1,8,48,48]{5,4,3,2,1,0:T(8,128)(2,1)S(1)}, bf16[8,1,1,8,48,48]{5,4,3,2,1,0:T(8,128)(2,1)}, u32[]{:S(2)}) copy-start(bf16[8,1,1,8,48,48]{5,4,3,2,1,0:T(8,128)(2,1)} %param.13) | copy-start | bytes 884740
  29.0 9.4 %collective-permute-start.7 = (f32[8,48]{1,0:T(8,128)S(1)}, f32[8,48]{1,0:T(8,128)S(1)}, u32[]{:S(2)}, u32[]{:S(2)}) collective-permute-start(f32[8,48]{1,0:T(8,128)S(1)} %get-tuple-element.29.approx_ref), channel_id=1, source_target_pairs={{0,1008},{16,32},{32,16},{48,64},{64,48},{80,96},{96,80},{112,128}... | collective-permute-start | bytes 4616 | tf_op jit(solution)/shard_map/ppermute | solution.py:365
  36.0 5.5 %collective-permute-start.6 = (f32[8,48]{1,0:T(8,128)S(1)}, f32[8,48]{1,0:T(8,128)S(1)}, u32[]{:S(2)}, u32[]{:S(2)}) collective-permute-start(f32[8,48]{1,0:T(8,128)S(1)} %get-tuple-element.29.approx_ref), channel_id=1, source_target_pairs={{0,16},{16,0},{32,48},{48,32},{64,80},{80,64},{96,112},{112,96},{1... | collective-permute-start | bytes 4616 | tf_op jit(solution)/shard_map/ppermute | solution.py:365
  37.9 3.6 %collective-permute-start.5 = (f32[8,48]{1,0:T(8,128)S(1)}, f32[8,48]{1,0:T(8,128)S(1)}, u32[]{:S(2)}, u32[]{:S(2)}) collective-permute-start(f32[8,48]{1,0:T(8,128)S(1)} %get-tuple-element.29.approx_ref), channel_id=1, source_target_pairs={{0,15},{1,0},{2,1},{3,2},{4,3},{5,4},{6,5},{7,6},{8,7},{9,8},{10,9... | collective-permute-start | bytes 4616 | tf_op jit(solution)/shard_map/ppermute | solution.py:360
  37.9 4.3 %collective-permute-start.4 = (f32[8,48]{1,0:T(8,128)S(1)}, f32[8,48]{1,0:T(8,128)S(1)}, u32[]{:S(2)}, u32[]{:S(2)}) collective-permute-start(f32[8,48]{1,0:T(8,128)S(1)} %get-tuple-element.29.approx_ref), channel_id=1, source_target_pairs={{0,1},{1,2},{2,3},{3,4},{4,5},{5,6},{6,7},{7,8},{8,9},{9,10},{10,1... | collective-permute-start | bytes 4616 | tf_op jit(solution)/shard_map/ppermute | solution.py:360
  42.7 8.8 %collective-permute-start.11 = (f32[8,48]{1,0:T(8,128)S(1)}, f32[8,48]{1,0:T(8,128)S(1)}, u32[]{:S(2)}, u32[]{:S(2)}) collective-permute-start(f32[8,48]{1,0:T(8,128)S(1)} %shard_map.89.approx_ref), channel_id=1, source_target_pairs={{0,1008},{16,32},{32,16},{48,64},{64,48},{80,96},{96,80},{112,128}... | collective-permute-start | bytes 4616 | tf_op jit(solution)/shard_map/ppermute | solution.py:365
  45.4 6.2 %collective-permute-start.10 = (f32[8,48]{1,0:T(8,128)S(1)}, f32[8,48]{1,0:T(8,128)S(1)}, u32[]{:S(2)}, u32[]{:S(2)}) collective-permute-start(f32[8,48]{1,0:T(8,128)S(1)} %shard_map.89.approx_ref), channel_id=1, source_target_pairs={{0,16},{16,0},{32,48},{48,32},{64,80},{80,64},{96,112},{112,96},{1... | collective-permute-start | bytes 4616 | tf_op jit(solution)/shard_map/ppermute | solution.py:365
  48.6 3.0 %collective-permute-start.9 = (f32[8,48]{1,0:T(8,128)S(1)}, f32[8,48]{1,0:T(8,128)S(1)}, u32[]{:S(2)}, u32[]{:S(2)}) collective-permute-start(f32[8,48]{1,0:T(8,128)S(1)} %shard_map.89.approx_ref), channel_id=1, source_target_pairs={{0,15},{1,0},{2,1},{3,2},{4,3},{5,4},{6,5},{7,6},{8,7},{9,8},{10,9... | collective-permute-start | bytes 4616 | tf_op jit(solution)/shard_map/ppermute | solution.py:360
  48.6 4.3 %collective-permute-start.8 = (f32[8,48]{1,0:T(8,128)S(1)}, f32[8,48]{1,0:T(8,128)S(1)}, u32[]{:S(2)}, u32[]{:S(2)}) collective-permute-start(f32[8,48]{1,0:T(8,128)S(1)} %shard_map.89.approx_ref), channel_id=1, source_target_pairs={{0,1},{1,2},{2,3},{3,4},{4,5},{5,6},{6,7},{7,8},{8,9},{9,10},{10,1... | collective-permute-start | bytes 4616 | tf_op jit(solution)/shard_map/ppermute | solution.py:360
  54.2 12.9 %collective-permute-start.12 = (f32[24,128]{1,0:T(8,128)S(1)}, f32[24,128]{1,0:T(8,128)S(1)}, u32[]{:S(2)}, u32[]{:S(2)}) collective-permute-start(f32[24,128]{1,0:T(8,128)S(1)} %get-tuple-element.36), channel_id=1, source_target_pairs={{0,1},{1,2},{2,3},{3,4},{4,5},{5,6},{6,7},{7,8},{8,9},{9,10},{10,1... | collective-permute-start | bytes 36872 | tf_op jit(solution)/shard_map/ppermute | solution.py:360
  54.3 12.8 %collective-permute-start.13 = (f32[24,128]{1,0:T(8,128)S(1)}, f32[24,128]{1,0:T(8,128)S(1)}, u32[]{:S(2)}, u32[]{:S(2)}) collective-permute-start(f32[24,128]{1,0:T(8,128)S(1)} %get-tuple-element.37), channel_id=1, source_target_pairs={{0,15},{1,0},{2,1},{3,2},{4,3},{5,4},{6,5},{7,6},{8,7},{9,8},{10,9... | collective-permute-start | bytes 36872 | tf_op jit(solution)/shard_map/ppermute | solution.py:360
  57.2 9.9 %collective-permute-start.14 = (f32[24,128]{1,0:T(8,128)S(1)}, f32[24,128]{1,0:T(8,128)S(1)}, u32[]{:S(2)}, u32[]{:S(2)}) collective-permute-start(f32[24,128]{1,0:T(8,128)S(1)} %get-tuple-element.38), channel_id=1, source_target_pairs={{0,16},{16,0},{32,48},{48,32},{64,80},{80,64},{96,112},{112,96},{1... | collective-permute-start | bytes 36872 | tf_op jit(solution)/shard_map/ppermute | solution.py:365
  59.8 8.9 %collective-permute-start.15 = (f32[24,128]{1,0:T(8,128)S(1)}, f32[24,128]{1,0:T(8,128)S(1)}, u32[]{:S(2)}, u32[]{:S(2)}) collective-permute-start(f32[24,128]{1,0:T(8,128)S(1)} %get-tuple-element.39), channel_id=1, source_target_pairs={{0,1008},{16,32},{32,16},{48,64},{64,48},{80,96},{96,80},{112,128}... | collective-permute-start | bytes 36872 | tf_op jit(solution)/shard_map/ppermute | solution.py:365

commit v3 on v2

--- a/solution.py
+++ b/solution.py
@@ -269,7 +269,7 @@
 
 
 def restrict_kernel(
-    odd_ref, inside_ref, links_ref, x_back, x_ahead, t_first, t_second, null_ref, inverse_ref, coarse_ref, approx_ref, summed_ref
+    odd_ref, inside_ref, links_ref, t_second, t_first, x_ahead, x_back, null_ref, inverse_ref, coarse_ref, approx_ref, summed_ref
 ):
     residual = residual_tiles(odd_ref, inside_ref, links_ref, x_back, x_ahead, t_first, t_second)
     rough = [r.astype(jnp.bfloat16).astype(jnp.float32) for r in residual]
@@ -333,7 +333,7 @@
     write_faces(updated, links_ref, odd_ref[0] == 1, (t_first, t_second, x_up, x_down), work_ref)
 
 
-def residual_kernel(odd_ref, inside_ref, links_ref, x_back, x_ahead, t_first, t_second, out_ref):
+def residual_kernel(odd_ref, inside_ref, links_ref, t_second, t_first, x_ahead, x_back, out_ref):
     residual = residual_tiles(odd_ref, inside_ref, links_ref, x_back, x_ahead, t_first, t_second)
     for m in range(12):
         out_ref[m] = residual[m]
@@ -414,7 +414,7 @@
         cost=beside,
     )
     rhs, approx = call(
-        restrict_kernel, [coarse, coarse], [sums], odd, inside, link_tiles, *halos, null_tiles, inverse
+        restrict_kernel, [coarse, coarse], [sums], odd, inside, link_tiles, *halos[::-1], null_tiles, inverse
     )
     for _ in range(SWEEPS - 1):
         near = swapped(approx, approx, approx, approx)
@@ -436,7 +436,7 @@
     )
     halos = swapped(x_up, x_down, t_first, t_second)
     inside, updated = call(inside_kernel, [tiles, tiles], [], updated, link_tiles, right, clover_tiles, cost=beside)
-    (after,) = call(residual_kernel, [tiles], [], odd, inside, link_tiles, *halos)
+    (after,) = call(residual_kernel, [tiles], [], odd, inside, link_tiles, *halos[::-1])
     return updated.reshape(shape), after.reshape(shape)
 
 

time: 69.8 us -> 65.4 us (0.937)
  the two profiles are of different devices: /device:TPU:64 before, /device:TPU:128 now
where the time goes in v3:
time: 65.4 us; the launch traced here: 65.1 us
  starting transfers between devices  44.1 us (67%)
  waiting for transfers between devices  13 us (20%)
  Pallas kernels  7.1 us (11%)
  between operations  0.78 us (1%)
    ppermute x8, starting transfers between devices, traded(): lax.ppermute(value, axis, [(i, (i + (1 if i % 2 == second else -1)) % siz...  39.4 us
    ppermute x8, waiting for transfers between devices, moved(): lax.ppermute(value, axis, [(i, (i + step) % size) for i in range(size)])  8.8 us
    pallas_call x7, Pallas kernels, call(): pl.pallas_call(kernel, out_shape=[jax.ShapeDtypeStruct(*out) for out in o...  7.1 us
    ppermute x8, starting transfers between devices, moved(): lax.ppermute(value, axis, [(i, (i + step) % size) for i in range(size)])  4.71 us
    ppermute x8, waiting for transfers between devices, traded(): lax.ppermute(value, axis, [(i, (i + (1 if i % 2 == second else -1)) % siz...  4.24 us
  transfers between devices with their start and end apart: 16, of which 8 were waited for; matrix products, arithmetic and copies ran while one was open for 0% of the time, Pallas kernels for 4%

profile of v3, /device:TPU:128, one launch (start us, length us, event | category | flops | bytes accessed | tf_op | source)
XLA Modules:
  0.0 65.1 jit_solution(9728980516883630454)
XLA Ops:
  0.6 0.0 copy-start.1
  0.7 1.0 %shard_map.86 = (f32[12,16,128]{2,1,0:T(8,128)S(1)}, bf16[36,16,128]{2,1,0:T(8,128)(2,1)S(1)}, f32[24,128]{1,0:T(8,128)S(1)}, f32[24,128]{1,0:T(8,128)S(1)}, f32...) custom-call(s32[1]{0:T(128)} %bitcast.odd_ref, f32[12,16,128]{2,1,0:T(8,128)} %bitcast.19, bf16[36,16,128]{2,1,0:T(8,128)(2,1)} %bitcast.17), custom_call_target="tpu_custom_call" | custom-call | tf_op jit(solution)/shard_map/pallas_call | solution.py:347
  1.7 5.2 %collective-permute-start = (f32[24,128]{1,0:T(8,128)S(1)}, f32[24,128]{1,0:T(8,128)S(1)}, u32[]{:S(2)}, u32[]{:S(2)}) collective-permute-start(f32[24,128]{1,0:T(8,128)S(1)} %get-tuple-element.24), channel_id=1, source_target_pairs={{0,1008},{16,32},{32,16},{48,64},{64,48},{80,96},{96,80},{112,128}... | collective-permute-start | bytes 36872 | tf_op jit(solution)/shard_map/ppermute | solution.py:365
  6.9 15.1 %collective-permute-start.1 = (f32[24,128]{1,0:T(8,128)S(1)}, f32[24,128]{1,0:T(8,128)S(1)}, u32[]{:S(2)}, u32[]{:S(2)}) collective-permute-start(f32[24,128]{1,0:T(8,128)S(1)} %get-tuple-element.25), channel_id=1, source_target_pairs={{0,16},{16,0},{32,48},{48,32},{64,80},{80,64},{96,112},{112,96},{1... | collective-permute-start | bytes 36872 | tf_op jit(solution)/shard_map/ppermute | solution.py:365
  22.0 3.2 %collective-permute-start.2 = (f32[24,128]{1,0:T(8,128)S(1)}, f32[24,128]{1,0:T(8,128)S(1)}, u32[]{:S(2)}, u32[]{:S(2)}) collective-permute-start(f32[24,128]{1,0:T(8,128)S(1)} %get-tuple-element.26), channel_id=1, source_target_pairs={{0,15},{1,0},{2,1},{3,2},{4,3},{5,4},{6,5},{7,6},{8,7},{9,8},{10,9... | collective-permute-start | bytes 36872 | tf_op jit(solution)/shard_map/ppermute | solution.py:360
  25.2 0.0 collective-permute-start.3
  25.2 0.0 copy-start
  25.2 1.9 %shard_map.87 = (f32[12,16,128]{2,1,0:T(8,128)S(1)}, f32[12,16,128]{2,1,0:T(8,128)S(1)}, bf16[72,16,128]{2,1,0:T(8,128)(2,1)S(1)}, bf16[576,16,128]{2,1,0:T(8,128)(2,1)S(1)}) custom-call(f32[12,16,128]{2,1,0:T(8,128)S(1)} %get-tuple-element.21.field_ref, bf16[36,16,128]{2,1,0:T(8,128)(2,1)S(1)} %get-tuple-element.22.links_ref, f32[12,16,128]{2,1,0:T(8,128)} %bitcast.18, ...), custom_call_target="tpu_custom_call" | custom-call | flops 4000000 | bytes 6000000 | tf_op jit(solution)/shard_map/pallas_call | solution.py:347
  27.1 0.0 collective-permute-done.t_second
  27.1 0.0 collective-permute-done.1.t_first
  27.1 0.0 collective-permute-done.2.x_ahead
  27.1 2.4 %collective-permute-done.3.x_back = f32[24,128]{1,0:T(8,128)S(1)} collective-permute-done((f32[24,128]{1,0:T(8,128)S(1)}, f32[24,128]{1,0:T(8,128)S(1)}, u32[]{:S(2)}, u32[]{:S(2)}) %collective-permute-start.3) | collective-permute-done | bytes 12320 | tf_op jit(solution)/shard_map/ppermute | solution.py:360
  29.5 0.0 copy-done.1
  29.5 0.8 %shard_map.88 = (f32[8,48]{1,0:T(8,128)S(1)}, f32[8,48]{1,0:T(8,128)S(1)}) custom-call(s32[1]{0:T(128)} %bitcast.odd_ref, f32[12,16,128]{2,1,0:T(8,128)S(1)} %get-tuple-element.23.inside_ref, bf16[36,16,128]{2,1,0:T(8,128)(2,1)S(1)} %get-tuple-element.22.links_ref, f32[24,128]{1,0:T(8,128)S(1)} %collective-permute-done.t_second, ...), custom_call_target="tpu_custom_call" | custom-call | tf_op jit(solution)/shard_map/pallas_call | solution.py:347
  30.3 1.9 %collective-permute-start.7 = (f32[8,48]{1,0:T(8,128)S(1)}, f32[8,48]{1,0:T(8,128)S(1)}, u32[]{:S(2)}, u32[]{:S(2)}) collective-permute-start(f32[8,48]{1,0:T(8,128)S(1)} %get-tuple-element.29.approx_ref), channel_id=1, source_target_pairs={{0,1008},{16,32},{32,16},{48,64},{64,48},{80,96},{96,80},{112,128}... | collective-permute-start | bytes 4616 | tf_op jit(solution)/shard_map/ppermute | solution.py:365
  32.3 2.5 %collective-permute-start.6 = (f32[8,48]{1,0:T(8,128)S(1)}, f32[8,48]{1,0:T(8,128)S(1)}, u32[]{:S(2)}, u32[]{:S(2)}) collective-permute-start(f32[8,48]{1,0:T(8,128)S(1)} %get-tuple-element.29.approx_ref), channel_id=1, source_target_pairs={{0,16},{16,0},{32,48},{48,32},{64,80},{80,64},{96,112},{112,96},{1... | collective-permute-start | bytes 4616 | tf_op jit(solution)/shard_map/ppermute | solution.py:365
  34.7 0.0 collective-permute-start.5
  34.8 0.5 collective-permute-start.4
  35.3 0.6 collective-permute-done.7.t_second
  35.8 1.9 %collective-permute-done.6.t_first = f32[8,48]{1,0:T(8,128)S(1)} collective-permute-done((f32[8,48]{1,0:T(8,128)S(1)}, f32[8,48]{1,0:T(8,128)S(1)}, u32[]{:S(2)}, u32[]{:S(2)}) %collective-permute-start.6) | collective-permute-done | bytes 1568 | tf_op jit(solution)/shard_map/ppermute | solution.py:365
  37.8 0.0 collective-permute-done.5.x_ahead
  37.8 1.3 %collective-permute-done.4.x_back = f32[8,48]{1,0:T(8,128)S(1)} collective-permute-done((f32[8,48]{1,0:T(8,128)S(1)}, f32[8,48]{1,0:T(8,128)S(1)}, u32[]{:S(2)}, u32[]{:S(2)}) %collective-permute-start.4) | collective-permute-done | bytes 1568 | tf_op jit(solution)/shard_map/ppermute | solution.py:360
  39.0 0.0 copy-done
  39.0 0.6 shard_map.89.approx_ref
  39.6 3.7 %collective-permute-start.11 = (f32[8,48]{1,0:T(8,128)S(1)}, f32[8,48]{1,0:T(8,128)S(1)}, u32[]{:S(2)}, u32[]{:S(2)}) collective-permute-start(f32[8,48]{1,0:T(8,128)S(1)} %shard_map.89.approx_ref), channel_id=1, source_target_pairs={{0,1008},{16,32},{32,16},{48,64},{64,48},{80,96},{96,80},{112,128}... | collective-permute-start | bytes 4616 | tf_op jit(solution)/shard_map/ppermute | solution.py:365
  43.2 5.5 %collective-permute-start.10 = (f32[8,48]{1,0:T(8,128)S(1)}, f32[8,48]{1,0:T(8,128)S(1)}, u32[]{:S(2)}, u32[]{:S(2)}) collective-permute-start(f32[8,48]{1,0:T(8,128)S(1)} %shard_map.89.approx_ref), channel_id=1, source_target_pairs={{0,16},{16,0},{32,48},{48,32},{64,80},{80,64},{96,112},{112,96},{1... | collective-permute-start | bytes 4616 | tf_op jit(solution)/shard_map/ppermute | solution.py:365
  48.8 0.0 collective-permute-start.9
  48.8 0.5 collective-permute-start.8
  49.3 0.0 collective-permute-done.11.t_ahead
  49.3 1.0 %collective-permute-done.10.t_back = f32[8,48]{1,0:T(8,128)S(1)} collective-permute-done((f32[8,48]{1,0:T(8,128)S(1)}, f32[8,48]{1,0:T(8,128)S(1)}, u32[]{:S(2)}, u32[]{:S(2)}) %collective-permute-start.10) | collective-permute-done | bytes 1568 | tf_op jit(solution)/shard_map/ppermute | solution.py:365
  50.3 0.0 collective-permute-done.9.x_ahead
  50.3 2.7 %collective-permute-done.8.x_back = f32[8,48]{1,0:T(8,128)S(1)} collective-permute-done((f32[8,48]{1,0:T(8,128)S(1)}, f32[8,48]{1,0:T(8,128)S(1)}, u32[]{:S(2)}, u32[]{:S(2)}) %collective-permute-start.8) | collective-permute-done | bytes 1568 | tf_op jit(solution)/shard_map/ppermute | solution.py:360
  53.1 1.3 %shard_map.90 = (f32[12,16,128]{2,1,0:T(8,128)S(1)}, f32[24,128]{1,0:T(8,128)S(1)}, f32[24,128]{1,0:T(8,128)S(1)}, f32[24,128]{1,0:T(8,128)S(1)}, f32[24,128]{1,0:T(8,128)S(1)}) custom-call(s32[1]{0:T(128)} %bitcast.odd_ref, f32[8,48]{1,0:T(8,128)S(1)} %shard_map.89.approx_ref, f32[8,48]{1,0:T(8,128)S(1)} %get-tuple-element.30.rhs_ref, ...), custom_call_target="tpu_custom_call" | custom-call | tf_op jit(solution)/shard_map/pallas_call | solution.py:347
  54.4 1.9 %collective-permute-start.12 = (f32[24,128]{1,0:T(8,128)S(1)}, f32[24,128]{1,0:T(8,128)S(1)}, u32[]{:S(2)}, u32[]{:S(2)}) collective-permute-start(f32[24,128]{1,0:T(8,128)S(1)} %get-tuple-element.36), channel_id=1, source_target_pairs={{0,1008},{16,32},{32,16},{48,64},{64,48},{80,96},{96,80},{112,128}... | collective-permute-start | bytes 36872 | tf_op jit(solution)/shard_map/ppermute | solution.py:365
  56.3 3.6 %collective-permute-start.13 = (f32[24,128]{1,0:T(8,128)S(1)}, f32[24,128]{1,0:T(8,128)S(1)}, u32[]{:S(2)}, u32[]{:S(2)}) collective-permute-start(f32[24,128]{1,0:T(8,128)S(1)} %get-tuple-element.37), channel_id=1, source_target_pairs={{0,16},{16,0},{32,48},{48,32},{64,80},{80,64},{96,112},{112,96},{1... | collective-permute-start | bytes 36872 | tf_op jit(solution)/shard_map/ppermute | solution.py:365
  60.0 0.0 collective-permute-start.14
  60.0 0.5 collective-permute-start.15
  60.5 0.7 %shard_map.91 = (f32[12,16,128]{2,1,0:T(8,128)S(1)}, f32[12,16,128]{2,1,0:T(8,128)}) custom-call(f32[12,16,128]{2,1,0:T(8,128)S(1)} %get-tuple-element.31.field_ref, bf16[36,16,128]{2,1,0:T(8,128)(2,1)S(1)} %get-tuple-element.22.links_ref, f32[12,16,128]{2,1,0:T(8,128)S(1)} %get-tuple-element.32.right_ref, bf16[72,16,128]{2,1,0:T(8,128)(2,1)S(1)} %get-tuple-element.33.clover_ref), custom_call_target="tpu_custom_call" | custom-call | flops 4000000 | bytes 6000000 | tf_op jit(solution)/shard_map/pallas_call | solution.py:347
  61.2 0.0 collective-permute-done.12.t_second
  61.2 0.7 %collective-permute-done.13.t_first = f32[24,128]{1,0:T(8,128)S(1)} collective-permute-done((f32[24,128]{1,0:T(8,128)S(1)}, f32[24,128]{1,0:T(8,128)S(1)}, u32[]{:S(2)}, u32[]{:S(2)}) %collective-permute-start.13) | collective-permute-done | bytes 12320 | tf_op jit(solution)/shard_map/ppermute | solution.py:365
  61.9 0.0 collective-permute-done.14.x_ahead
  61.9 2.4 %collective-permute-done.15.x_back = f32[24,128]{1,0:T(8,128)S(1)} collective-permute-done((f32[24,128]{1,0:T(8,128)S(1)}, f32[24,128]{1,0:T(8,128)S(1)}, u32[]{:S(2)}, u32[]{:S(2)}) %collective-permute-start.15) | collective-permute-done | bytes 12320 | tf_op jit(solution)/shard_map/ppermute | solution.py:360
  64.3 0.7 %shard_map.92 = f32[12,16,128]{2,1,0:T(8,128)} custom-call(s32[1]{0:T(128)} %bitcast.odd_ref, f32[12,16,128]{2,1,0:T(8,128)S(1)} %get-tuple-element.35.inside_ref, bf16[36,16,128]{2,1,0:T(8,128)(2,1)S(1)} %get-tuple-element.22.links_ref, f32[24,128]{1,0:T(8,128)S(1)} %collective-permute-done.12.t_second, f32[24,128]{1,0:T(8,128)S(1)} %collective-permute-done.13.t_first, ...), custom_call_target="tpu_custom_call" | custom-call | tf_op jit(solution)/shard_map/pallas_call | solution.py:347
Async XLA Ops:
  0.6 28.9 %copy-start.1 = (bf16[1,1,8,48,48]{4,3,2,1,0:T(8,128)(2,1)S(1)}, bf16[1,1,8,48,48]{4,3,2,1,0:T(8,128)(2,1)}, u32[]{:S(2)}) copy-start(bf16[1,1,8,48,48]{4,3,2,1,0:T(8,128)(2,1)} %param.12) | copy-start | bytes 110596
  1.7 25.4 %collective-permute-start = (f32[24,128]{1,0:T(8,128)S(1)}, f32[24,128]{1,0:T(8,128)S(1)}, u32[]{:S(2)}, u32[]{:S(2)}) collective-permute-start(f32[24,128]{1,0:T(8,128)S(1)} %get-tuple-element.24), channel_id=1, source_target_pairs={{0,1008},{16,32},{32,16},{48,64},{64,48},{80,96},{96,80},{112,128}... | collective-permute-start | bytes 36872 | tf_op jit(solution)/shard_map/ppermute | solution.py:365
  6.9 20.2 %collective-permute-start.1 = (f32[24,128]{1,0:T(8,128)S(1)}, f32[24,128]{1,0:T(8,128)S(1)}, u32[]{:S(2)}, u32[]{:S(2)}) collective-permute-start(f32[24,128]{1,0:T(8,128)S(1)} %get-tuple-element.25), channel_id=1, source_target_pairs={{0,16},{16,0},{32,48},{48,32},{64,80},{80,64},{96,112},{112,96},{1... | collective-permute-start | bytes 36872 | tf_op jit(solution)/shard_map/ppermute | solution.py:365
  22.0 5.1 %collective-permute-start.2 = (f32[24,128]{1,0:T(8,128)S(1)}, f32[24,128]{1,0:T(8,128)S(1)}, u32[]{:S(2)}, u32[]{:S(2)}) collective-permute-start(f32[24,128]{1,0:T(8,128)S(1)} %get-tuple-element.26), channel_id=1, source_target_pairs={{0,15},{1,0},{2,1},{3,2},{4,3},{5,4},{6,5},{7,6},{8,7},{9,8},{10,9... | collective-permute-start | bytes 36872 | tf_op jit(solution)/shard_map/ppermute | solution.py:360
  25.2 4.3 %collective-permute-start.3 = (f32[24,128]{1,0:T(8,128)S(1)}, f32[24,128]{1,0:T(8,128)S(1)}, u32[]{:S(2)}, u32[]{:S(2)}) collective-permute-start(f32[24,128]{1,0:T(8,128)S(1)} %get-tuple-element.27), channel_id=1, source_target_pairs={{0,1},{1,2},{2,3},{3,4},{4,5},{5,6},{6,7},{7,8},{8,9},{9,10},{10,1... | collective-permute-start | bytes 36872 | tf_op jit(solution)/shard_map/ppermute | solution.py:360
  25.2 13.9 %copy-start = (bf16[8,1,1,8,48,48]{5,4,3,2,1,0:T(8,128)(2,1)S(1)}, bf16[8,1,1,8,48,48]{5,4,3,2,1,0:T(8,128)(2,1)}, u32[]{:S(2)}) copy-start(bf16[8,1,1,8,48,48]{5,4,3,2,1,0:T(8,128)(2,1)} %param.13) | copy-start | bytes 884740
  30.3 5.5 %collective-permute-start.7 = (f32[8,48]{1,0:T(8,128)S(1)}, f32[8,48]{1,0:T(8,128)S(1)}, u32[]{:S(2)}, u32[]{:S(2)}) collective-permute-start(f32[8,48]{1,0:T(8,128)S(1)} %get-tuple-element.29.approx_ref), channel_id=1, source_target_pairs={{0,1008},{16,32},{32,16},{48,64},{64,48},{80,96},{96,80},{112,128}... | collective-permute-start | bytes 4616 | tf_op jit(solution)/shard_map/ppermute | solution.py:365
  32.3 5.5 %collective-permute-start.6 = (f32[8,48]{1,0:T(8,128)S(1)}, f32[8,48]{1,0:T(8,128)S(1)}, u32[]{:S(2)}, u32[]{:S(2)}) collective-permute-start(f32[8,48]{1,0:T(8,128)S(1)} %get-tuple-element.29.approx_ref), channel_id=1, source_target_pairs={{0,16},{16,0},{32,48},{48,32},{64,80},{80,64},{96,112},{112,96},{1... | collective-permute-start | bytes 4616 | tf_op jit(solution)/shard_map/ppermute | solution.py:365
  34.7 3.0 %collective-permute-start.5 = (f32[8,48]{1,0:T(8,128)S(1)}, f32[8,48]{1,0:T(8,128)S(1)}, u32[]{:S(2)}, u32[]{:S(2)}) collective-permute-start(f32[8,48]{1,0:T(8,128)S(1)} %get-tuple-element.29.approx_ref), channel_id=1, source_target_pairs={{0,15},{1,0},{2,1},{3,2},{4,3},{5,4},{6,5},{7,6},{8,7},{9,8},{10,9... | collective-permute-start | bytes 4616 | tf_op jit(solution)/shard_map/ppermute | solution.py:360
  34.8 4.2 %collective-permute-start.4 = (f32[8,48]{1,0:T(8,128)S(1)}, f32[8,48]{1,0:T(8,128)S(1)}, u32[]{:S(2)}, u32[]{:S(2)}) collective-permute-start(f32[8,48]{1,0:T(8,128)S(1)} %get-tuple-element.29.approx_ref), channel_id=1, source_target_pairs={{0,1},{1,2},{2,3},{3,4},{4,5},{5,6},{6,7},{7,8},{8,9},{9,10},{10,1... | collective-permute-start | bytes 4616 | tf_op jit(solution)/shard_map/ppermute | solution.py:360
  39.6 9.7 %collective-permute-start.11 = (f32[8,48]{1,0:T(8,128)S(1)}, f32[8,48]{1,0:T(8,128)S(1)}, u32[]{:S(2)}, u32[]{:S(2)}) collective-permute-start(f32[8,48]{1,0:T(8,128)S(1)} %shard_map.89.approx_ref), channel_id=1, source_target_pairs={{0,1008},{16,32},{32,16},{48,64},{64,48},{80,96},{96,80},{112,128}... | collective-permute-start | bytes 4616 | tf_op jit(solution)/shard_map/ppermute | solution.py:365
  43.2 7.1 %collective-permute-start.10 = (f32[8,48]{1,0:T(8,128)S(1)}, f32[8,48]{1,0:T(8,128)S(1)}, u32[]{:S(2)}, u32[]{:S(2)}) collective-permute-start(f32[8,48]{1,0:T(8,128)S(1)} %shard_map.89.approx_ref), channel_id=1, source_target_pairs={{0,16},{16,0},{32,48},{48,32},{64,80},{80,64},{96,112},{112,96},{1... | collective-permute-start | bytes 4616 | tf_op jit(solution)/shard_map/ppermute | solution.py:365
  48.8 1.6 %collective-permute-start.9 = (f32[8,48]{1,0:T(8,128)S(1)}, f32[8,48]{1,0:T(8,128)S(1)}, u32[]{:S(2)}, u32[]{:S(2)}) collective-permute-start(f32[8,48]{1,0:T(8,128)S(1)} %shard_map.89.approx_ref), channel_id=1, source_target_pairs={{0,15},{1,0},{2,1},{3,2},{4,3},{5,4},{6,5},{7,6},{8,7},{9,8},{10,9... | collective-permute-start | bytes 4616 | tf_op jit(solution)/shard_map/ppermute | solution.py:360
  48.8 4.3 %collective-permute-start.8 = (f32[8,48]{1,0:T(8,128)S(1)}, f32[8,48]{1,0:T(8,128)S(1)}, u32[]{:S(2)}, u32[]{:S(2)}) collective-permute-start(f32[8,48]{1,0:T(8,128)S(1)} %shard_map.89.approx_ref), channel_id=1, source_target_pairs={{0,1},{1,2},{2,3},{3,4},{4,5},{5,6},{6,7},{7,8},{8,9},{9,10},{10,1... | collective-permute-start | bytes 4616 | tf_op jit(solution)/shard_map/ppermute | solution.py:360
  54.4 6.8 %collective-permute-start.12 = (f32[24,128]{1,0:T(8,128)S(1)}, f32[24,128]{1,0:T(8,128)S(1)}, u32[]{:S(2)}, u32[]{:S(2)}) collective-permute-start(f32[24,128]{1,0:T(8,128)S(1)} %get-tuple-element.36), channel_id=1, source_target_pairs={{0,1008},{16,32},{32,16},{48,64},{64,48},{80,96},{96,80},{112,128}... | collective-permute-start | bytes 36872 | tf_op jit(solution)/shard_map/ppermute | solution.py:365
  56.3 5.6 %collective-permute-start.13 = (f32[24,128]{1,0:T(8,128)S(1)}, f32[24,128]{1,0:T(8,128)S(1)}, u32[]{:S(2)}, u32[]{:S(2)}) collective-permute-start(f32[24,128]{1,0:T(8,128)S(1)} %get-tuple-element.37), channel_id=1, source_target_pairs={{0,16},{16,0},{32,48},{48,32},{64,80},{80,64},{96,112},{112,96},{1... | collective-permute-start | bytes 36872 | tf_op jit(solution)/shard_map/ppermute | solution.py:365
  60.0 1.9 %collective-permute-start.14 = (f32[24,128]{1,0:T(8,128)S(1)}, f32[24,128]{1,0:T(8,128)S(1)}, u32[]{:S(2)}, u32[]{:S(2)}) collective-permute-start(f32[24,128]{1,0:T(8,128)S(1)} %get-tuple-element.38), channel_id=1, source_target_pairs={{0,15},{1,0},{2,1},{3,2},{4,3},{5,4},{6,5},{7,6},{8,7},{9,8},{10,9... | collective-permute-start | bytes 36872 | tf_op jit(solution)/shard_map/ppermute | solution.py:360
  60.0 4.3 %collective-permute-start.15 = (f32[24,128]{1,0:T(8,128)S(1)}, f32[24,128]{1,0:T(8,128)S(1)}, u32[]{:S(2)}, u32[]{:S(2)}) collective-permute-start(f32[24,128]{1,0:T(8,128)S(1)} %get-tuple-element.39), channel_id=1, source_target_pairs={{0,1},{1,2},{2,3},{3,4},{4,5},{5,6},{6,7},{7,8},{8,9},{9,10},{10,1... | collective-permute-start | bytes 36872 | tf_op jit(solution)/shard_map/ppermute | solution.py:360

commit v4 on v3

--- a/solution.py
+++ b/solution.py
@@ -262,14 +262,14 @@
 
 
 def sweep_kernel(
-    odd_ref, approx_ref, rhs_ref, x_back, x_ahead, t_first, t_second, couplings_ref, inverse_ref, out_ref
+    odd_ref, approx_ref, rhs_ref, t_first, x_back, x_ahead, t_second, couplings_ref, inverse_ref, out_ref
 ):
     near = (x_back, x_ahead, t_first, t_second)
     out_ref[...] = sweep(odd_ref[0] == 1, approx_ref, rhs_ref, near, couplings_ref, inverse_ref)
 
 
 def restrict_kernel(
-    odd_ref, inside_ref, links_ref, t_second, t_first, x_ahead, x_back, null_ref, inverse_ref, coarse_ref, approx_ref, summed_ref
+    odd_ref, inside_ref, links_ref, t_second, x_ahead, x_back, t_first, null_ref, inverse_ref, coarse_ref, approx_ref, summed_ref
 ):
     residual = residual_tiles(odd_ref, inside_ref, links_ref, x_back, x_ahead, t_first, t_second)
     rough = [r.astype(jnp.bfloat16).astype(jnp.float32) for r in residual]
@@ -296,9 +296,9 @@
     odd_ref,
     approx_ref,
     rhs_ref,
+    t_back,
     x_back,
     x_ahead,
-    t_back,
     t_ahead,
     couplings_ref,
     inverse_ref,
@@ -333,7 +333,7 @@
     write_faces(updated, links_ref, odd_ref[0] == 1, (t_first, t_second, x_up, x_down), work_ref)
 
 
-def residual_kernel(odd_ref, inside_ref, links_ref, t_second, t_first, x_ahead, x_back, out_ref):
+def residual_kernel(odd_ref, inside_ref, links_ref, t_second, x_ahead, x_back, t_first, out_ref):
     residual = residual_tiles(odd_ref, inside_ref, links_ref, x_back, x_ahead, t_first, t_second)
     for m in range(12):
         out_ref[m] = residual[m]
@@ -369,6 +369,10 @@
     return moved(x_up, "agg", 1), moved(x_down, "agg", -1), traded(t_first, "lat", 0), traded(t_second, "lat", 1)
 
 
+def by_start(x_back, x_ahead, t_first, t_second):
+    return t_second, x_ahead, x_back, t_first
+
+
 def shards(solution, right_side, links, clover, null_vectors, coarse_inverse, coarse_links):
     shape = solution.shape
     blocks, channels = coarse_inverse.shape[2], coarse_inverse.shape[-1]
@@ -414,11 +418,11 @@
         cost=beside,
     )
     rhs, approx = call(
-        restrict_kernel, [coarse, coarse], [sums], odd, inside, link_tiles, *halos[::-1], null_tiles, inverse
+        restrict_kernel, [coarse, coarse], [sums], odd, inside, link_tiles, *by_start(*halos), null_tiles, inverse
     )
     for _ in range(SWEEPS - 1):
         near = swapped(approx, approx, approx, approx)
-        (approx,) = call(sweep_kernel, [coarse], [], odd, approx, rhs, *near, couplings, inverse)
+        (approx,) = call(sweep_kernel, [coarse], [], odd, approx, rhs, *by_start(*near)[::-1], couplings, inverse)
     near = swapped(approx, approx, approx, approx)
     updated, t_first, t_second, x_up, x_down = call(
         prolong_kernel,
@@ -427,7 +431,7 @@
         odd,
         approx,
         rhs,
-        *near,
+        *by_start(*near)[::-1],
         couplings,
         inverse,
         field,
@@ -436,7 +440,7 @@
     )
     halos = swapped(x_up, x_down, t_first, t_second)
     inside, updated = call(inside_kernel, [tiles, tiles], [], updated, link_tiles, right, clover_tiles, cost=beside)
-    (after,) = call(residual_kernel, [tiles], [], odd, inside, link_tiles, *halos[::-1])
+    (after,) = call(residual_kernel, [tiles], [], odd, inside, link_tiles, *by_start(*halos))
     return updated.reshape(shape), after.reshape(shape)
 
 

time: 65.4 us -> 65.9 us (level)
  the two profiles are of different devices: /device:TPU:128 before, /device:TPU:49 now
where the time goes in v4:
time: 65.9 us; the launch traced here: 65 us
  starting transfers between devices  50.8 us (77%)
  Pallas kernels  7.11 us (11%)
  waiting for transfers between devices  6.23 us (9%)
  between operations  0.84 us (1%)
    ppermute x8, starting transfers between devices, traded(): lax.ppermute(value, axis, [(i, (i + (1 if i % 2 == second else -1)) % siz...  38.4 us
    ppermute x8, starting transfers between devices, moved(): lax.ppermute(value, axis, [(i, (i + step) % size) for i in range(size)])  12.4 us
    pallas_call x7, Pallas kernels, call(): pl.pallas_call(kernel, out_shape=[jax.ShapeDtypeStruct(*out) for out in o...  7.11 us
    ppermute x8, waiting for transfers between devices, traded(): lax.ppermute(value, axis, [(i, (i + (1 if i % 2 == second else -1)) % siz...  6.21 us
  transfers between devices with their start and end apart: 16, of which 5 were waited for; matrix products, arithmetic and copies ran while one was open for 0% of the time, Pallas kernels for 4%

profile of v4, /device:TPU:49, one launch (start us, length us, event | category | flops | bytes accessed | tf_op | source)
XLA Modules:
  0.0 65.0 jit_solution(5435800589250197917)
XLA Ops:
  0.6 0.0 copy-start.1
  0.7 1.0 %shard_map.86 = (f32[12,16,128]{2,1,0:T(8,128)S(1)}, bf16[36,16,128]{2,1,0:T(8,128)(2,1)S(1)}, f32[24,128]{1,0:T(8,128)S(1)}, f32[24,128]{1,0:T(8,128)S(1)}, f32...) custom-call(s32[1]{0:T(128)} %bitcast.odd_ref, f32[12,16,128]{2,1,0:T(8,128)} %bitcast.19, bf16[36,16,128]{2,1,0:T(8,128)(2,1)} %bitcast.17), custom_call_target="tpu_custom_call" | custom-call | tf_op jit(solution)/shard_map/pallas_call | solution.py:347
  1.7 19.3 %collective-permute-start = (f32[24,128]{1,0:T(8,128)S(1)}, f32[24,128]{1,0:T(8,128)S(1)}, u32[]{:S(2)}, u32[]{:S(2)}) collective-permute-start(f32[24,128]{1,0:T(8,128)S(1)} %get-tuple-element.24), channel_id=1, source_target_pairs={{0,1008},{16,32},{32,16},{48,64},{64,48},{80,96},{96,80},{112,128}... | collective-permute-start | bytes 36872 | tf_op jit(solution)/shard_map/ppermute | solution.py:365
  21.1 1.0 %collective-permute-start.1 = (f32[24,128]{1,0:T(8,128)S(1)}, f32[24,128]{1,0:T(8,128)S(1)}, u32[]{:S(2)}, u32[]{:S(2)}) collective-permute-start(f32[24,128]{1,0:T(8,128)S(1)} %get-tuple-element.25), channel_id=1, source_target_pairs={{0,15},{1,0},{2,1},{3,2},{4,3},{5,4},{6,5},{7,6},{8,7},{9,8},{10,9... | collective-permute-start | bytes 36872 | tf_op jit(solution)/shard_map/ppermute | solution.py:360
  22.0 2.5 %collective-permute-start.2 = (f32[24,128]{1,0:T(8,128)S(1)}, f32[24,128]{1,0:T(8,128)S(1)}, u32[]{:S(2)}, u32[]{:S(2)}) collective-permute-start(f32[24,128]{1,0:T(8,128)S(1)} %get-tuple-element.26), channel_id=1, source_target_pairs={{0,1},{1,2},{2,3},{3,4},{4,5},{5,6},{6,7},{7,8},{8,9},{9,10},{10,1... | collective-permute-start | bytes 36872 | tf_op jit(solution)/shard_map/ppermute | solution.py:360
  24.6 1.9 %collective-permute-start.3 = (f32[24,128]{1,0:T(8,128)S(1)}, f32[24,128]{1,0:T(8,128)S(1)}, u32[]{:S(2)}, u32[]{:S(2)}) collective-permute-start(f32[24,128]{1,0:T(8,128)S(1)} %get-tuple-element.27), channel_id=1, source_target_pairs={{0,16},{16,0},{32,48},{48,32},{64,80},{80,64},{96,112},{112,96},{1... | collective-permute-start | bytes 36872 | tf_op jit(solution)/shard_map/ppermute | solution.py:365
  26.5 0.0 copy-start
  26.5 1.9 %shard_map.87 = (f32[12,16,128]{2,1,0:T(8,128)S(1)}, f32[12,16,128]{2,1,0:T(8,128)S(1)}, bf16[72,16,128]{2,1,0:T(8,128)(2,1)S(1)}, bf16[576,16,128]{2,1,0:T(8,128)(2,1)S(1)}) custom-call(f32[12,16,128]{2,1,0:T(8,128)S(1)} %get-tuple-element.21.field_ref, bf16[36,16,128]{2,1,0:T(8,128)(2,1)S(1)} %get-tuple-element.22.links_ref, f32[12,16,128]{2,1,0:T(8,128)} %bitcast.18, ...), custom_call_target="tpu_custom_call" | custom-call | flops 4000000 | bytes 6000000 | tf_op jit(solution)/shard_map/pallas_call | solution.py:347
  28.4 0.0 collective-permute-done.t_second
  28.4 0.0 collective-permute-done.1.x_ahead
  28.4 0.0 collective-permute-done.2.x_back
  28.4 0.6 collective-permute-done.3.t_first
  29.0 0.0 copy-done.1
  29.0 0.8 %shard_map.88 = (f32[8,48]{1,0:T(8,128)S(1)}, f32[8,48]{1,0:T(8,128)S(1)}) custom-call(s32[1]{0:T(128)} %bitcast.odd_ref, f32[12,16,128]{2,1,0:T(8,128)S(1)} %get-tuple-element.23.inside_ref, bf16[36,16,128]{2,1,0:T(8,128)(2,1)S(1)} %get-tuple-element.22.links_ref, f32[24,128]{1,0:T(8,128)S(1)} %collective-permute-done.t_second, ...), custom_call_target="tpu_custom_call" | custom-call | tf_op jit(solution)/shard_map/pallas_call | solution.py:347
  29.8 1.9 %collective-permute-start.7 = (f32[8,48]{1,0:T(8,128)S(1)}, f32[8,48]{1,0:T(8,128)S(1)}, u32[]{:S(2)}, u32[]{:S(2)}) collective-permute-start(f32[8,48]{1,0:T(8,128)S(1)} %get-tuple-element.29.approx_ref), channel_id=1, source_target_pairs={{0,1008},{16,32},{32,16},{48,64},{64,48},{80,96},{96,80},{112,128}... | collective-permute-start | bytes 4616 | tf_op jit(solution)/shard_map/ppermute | solution.py:365
  31.7 0.0 collective-permute-start.6
  31.8 2.9 %collective-permute-start.5 = (f32[8,48]{1,0:T(8,128)S(1)}, f32[8,48]{1,0:T(8,128)S(1)}, u32[]{:S(2)}, u32[]{:S(2)}) collective-permute-start(f32[8,48]{1,0:T(8,128)S(1)} %get-tuple-element.29.approx_ref), channel_id=1, source_target_pairs={{0,1},{1,2},{2,3},{3,4},{4,5},{5,6},{6,7},{7,8},{8,9},{9,10},{10,1... | collective-permute-start | bytes 4616 | tf_op jit(solution)/shard_map/ppermute | solution.py:360
  34.7 2.8 %collective-permute-start.4 = (f32[8,48]{1,0:T(8,128)S(1)}, f32[8,48]{1,0:T(8,128)S(1)}, u32[]{:S(2)}, u32[]{:S(2)}) collective-permute-start(f32[8,48]{1,0:T(8,128)S(1)} %get-tuple-element.29.approx_ref), channel_id=1, source_target_pairs={{0,16},{16,0},{32,48},{48,32},{64,80},{80,64},{96,112},{112,96},{1... | collective-permute-start | bytes 4616 | tf_op jit(solution)/shard_map/ppermute | solution.py:365
  37.5 0.0 collective-permute-done.7.t_second
  37.6 0.0 collective-permute-done.6.x_ahead
  37.6 0.0 collective-permute-done.5.x_back
  37.6 1.5 %collective-permute-done.4.t_first = f32[8,48]{1,0:T(8,128)S(1)} collective-permute-done((f32[8,48]{1,0:T(8,128)S(1)}, f32[8,48]{1,0:T(8,128)S(1)}, u32[]{:S(2)}, u32[]{:S(2)}) %collective-permute-start.4) | collective-permute-done | bytes 1568 | tf_op jit(solution)/shard_map/ppermute | solution.py:365
  39.1 0.0 copy-done
  39.1 0.6 shard_map.89.approx_ref
  39.6 6.7 %collective-permute-start.11 = (f32[8,48]{1,0:T(8,128)S(1)}, f32[8,48]{1,0:T(8,128)S(1)}, u32[]{:S(2)}, u32[]{:S(2)}) collective-permute-start(f32[8,48]{1,0:T(8,128)S(1)} %shard_map.89.approx_ref), channel_id=1, source_target_pairs={{0,1008},{16,32},{32,16},{48,64},{64,48},{80,96},{96,80},{112,128}... | collective-permute-start | bytes 4616 | tf_op jit(solution)/shard_map/ppermute | solution.py:365
  46.3 0.0 collective-permute-start.10
  46.3 2.9 %collective-permute-start.9 = (f32[8,48]{1,0:T(8,128)S(1)}, f32[8,48]{1,0:T(8,128)S(1)}, u32[]{:S(2)}, u32[]{:S(2)}) collective-permute-start(f32[8,48]{1,0:T(8,128)S(1)} %shard_map.89.approx_ref), channel_id=1, source_target_pairs={{0,1},{1,2},{2,3},{3,4},{4,5},{5,6},{6,7},{7,8},{8,9},{9,10},{10,1... | collective-permute-start | bytes 4616 | tf_op jit(solution)/shard_map/ppermute | solution.py:360
  49.3 1.9 %collective-permute-start.8 = (f32[8,48]{1,0:T(8,128)S(1)}, f32[8,48]{1,0:T(8,128)S(1)}, u32[]{:S(2)}, u32[]{:S(2)}) collective-permute-start(f32[8,48]{1,0:T(8,128)S(1)} %shard_map.89.approx_ref), channel_id=1, source_target_pairs={{0,16},{16,0},{32,48},{48,32},{64,80},{80,64},{96,112},{112,96},{1... | collective-permute-start | bytes 4616 | tf_op jit(solution)/shard_map/ppermute | solution.py:365
  51.2 0.0 collective-permute-done.11.t_ahead
  51.2 0.0 collective-permute-done.10.x_ahead
  51.2 0.0 collective-permute-done.9.x_back
  51.2 2.4 %collective-permute-done.8.t_back = f32[8,48]{1,0:T(8,128)S(1)} collective-permute-done((f32[8,48]{1,0:T(8,128)S(1)}, f32[8,48]{1,0:T(8,128)S(1)}, u32[]{:S(2)}, u32[]{:S(2)}) %collective-permute-start.8) | collective-permute-done | bytes 1568 | tf_op jit(solution)/shard_map/ppermute | solution.py:365
  53.6 1.3 %shard_map.90 = (f32[12,16,128]{2,1,0:T(8,128)S(1)}, f32[24,128]{1,0:T(8,128)S(1)}, f32[24,128]{1,0:T(8,128)S(1)}, f32[24,128]{1,0:T(8,128)S(1)}, f32[24,128]{1,0:T(8,128)S(1)}) custom-call(s32[1]{0:T(128)} %bitcast.odd_ref, f32[8,48]{1,0:T(8,128)S(1)} %shard_map.89.approx_ref, f32[8,48]{1,0:T(8,128)S(1)} %get-tuple-element.30.rhs_ref, ...), custom_call_target="tpu_custom_call" | custom-call | tf_op jit(solution)/shard_map/pallas_call | solution.py:347
  55.0 1.9 %collective-permute-start.12 = (f32[24,128]{1,0:T(8,128)S(1)}, f32[24,128]{1,0:T(8,128)S(1)}, u32[]{:S(2)}, u32[]{:S(2)}) collective-permute-start(f32[24,128]{1,0:T(8,128)S(1)} %get-tuple-element.36), channel_id=1, source_target_pairs={{0,1008},{16,32},{32,16},{48,64},{64,48},{80,96},{96,80},{112,128}... | collective-permute-start | bytes 36872 | tf_op jit(solution)/shard_map/ppermute | solution.py:365
  56.9 0.0 collective-permute-start.13
  56.9 2.9 %collective-permute-start.14 = (f32[24,128]{1,0:T(8,128)S(1)}, f32[24,128]{1,0:T(8,128)S(1)}, u32[]{:S(2)}, u32[]{:S(2)}) collective-permute-start(f32[24,128]{1,0:T(8,128)S(1)} %get-tuple-element.38), channel_id=1, source_target_pairs={{0,1},{1,2},{2,3},{3,4},{4,5},{5,6},{6,7},{7,8},{8,9},{9,10},{10,1... | collective-permute-start | bytes 36872 | tf_op jit(solution)/shard_map/ppermute | solution.py:360
  59.9 1.9 %collective-permute-start.15 = (f32[24,128]{1,0:T(8,128)S(1)}, f32[24,128]{1,0:T(8,128)S(1)}, u32[]{:S(2)}, u32[]{:S(2)}) collective-permute-start(f32[24,128]{1,0:T(8,128)S(1)} %get-tuple-element.39), channel_id=1, source_target_pairs={{0,16},{16,0},{32,48},{48,32},{64,80},{80,64},{96,112},{112,96},{1... | collective-permute-start | bytes 36872 | tf_op jit(solution)/shard_map/ppermute | solution.py:365
  61.8 0.7 %shard_map.91 = (f32[12,16,128]{2,1,0:T(8,128)S(1)}, f32[12,16,128]{2,1,0:T(8,128)}) custom-call(f32[12,16,128]{2,1,0:T(8,128)S(1)} %get-tuple-element.31.field_ref, bf16[36,16,128]{2,1,0:T(8,128)(2,1)S(1)} %get-tuple-element.22.links_ref, f32[12,16,128]{2,1,0:T(8,128)S(1)} %get-tuple-element.32.right_ref, bf16[72,16,128]{2,1,0:T(8,128)(2,1)S(1)} %get-tuple-element.33.clover_ref), custom_call_target="tpu_custom_call" | custom-call | flops 4000000 | bytes 6000000 | tf_op jit(solution)/shard_map/pallas_call | solution.py:347
  62.5 0.2 collective-permute-done.12.t_second
  62.7 0.0 collective-permute-done.13.x_ahead
  62.7 0.0 collective-permute-done.14.x_back
  62.7 1.6 %collective-permute-done.15.t_first = f32[24,128]{1,0:T(8,128)S(1)} collective-permute-done((f32[24,128]{1,0:T(8,128)S(1)}, f32[24,128]{1,0:T(8,128)S(1)}, u32[]{:S(2)}, u32[]{:S(2)}) %collective-permute-start.15) | collective-permute-done | bytes 12320 | tf_op jit(solution)/shard_map/ppermute | solution.py:365
  64.3 0.7 %shard_map.92 = f32[12,16,128]{2,1,0:T(8,128)} custom-call(s32[1]{0:T(128)} %bitcast.odd_ref, f32[12,16,128]{2,1,0:T(8,128)S(1)} %get-tuple-element.35.inside_ref, bf16[36,16,128]{2,1,0:T(8,128)(2,1)S(1)} %get-tuple-element.22.links_ref, f32[24,128]{1,0:T(8,128)S(1)} %collective-permute-done.12.t_second, f32[24,128]{1,0:T(8,128)S(1)} %collective-permute-done.13.x_ahead, ...), custom_call_target="tpu_custom_call" | custom-call | tf_op jit(solution)/shard_map/pallas_call | solution.py:347
Async XLA Ops:
  0.6 28.4 %copy-start.1 = (bf16[1,1,8,48,48]{4,3,2,1,0:T(8,128)(2,1)S(1)}, bf16[1,1,8,48,48]{4,3,2,1,0:T(8,128)(2,1)}, u32[]{:S(2)}) copy-start(bf16[1,1,8,48,48]{4,3,2,1,0:T(8,128)(2,1)} %param.12) | copy-start | bytes 110596
  1.7 26.7 %collective-permute-start = (f32[24,128]{1,0:T(8,128)S(1)}, f32[24,128]{1,0:T(8,128)S(1)}, u32[]{:S(2)}, u32[]{:S(2)}) collective-permute-start(f32[24,128]{1,0:T(8,128)S(1)} %get-tuple-element.24), channel_id=1, source_target_pairs={{0,1008},{16,32},{32,16},{48,64},{64,48},{80,96},{96,80},{112,128}... | collective-permute-start | bytes 36872 | tf_op jit(solution)/shard_map/ppermute | solution.py:365
  21.1 7.4 %collective-permute-start.1 = (f32[24,128]{1,0:T(8,128)S(1)}, f32[24,128]{1,0:T(8,128)S(1)}, u32[]{:S(2)}, u32[]{:S(2)}) collective-permute-start(f32[24,128]{1,0:T(8,128)S(1)} %get-tuple-element.25), channel_id=1, source_target_pairs={{0,15},{1,0},{2,1},{3,2},{4,3},{5,4},{6,5},{7,6},{8,7},{9,8},{10,9... | collective-permute-start | bytes 36872 | tf_op jit(solution)/shard_map/ppermute | solution.py:360
  22.0 6.4 %collective-permute-start.2 = (f32[24,128]{1,0:T(8,128)S(1)}, f32[24,128]{1,0:T(8,128)S(1)}, u32[]{:S(2)}, u32[]{:S(2)}) collective-permute-start(f32[24,128]{1,0:T(8,128)S(1)} %get-tuple-element.26), channel_id=1, source_target_pairs={{0,1},{1,2},{2,3},{3,4},{4,5},{5,6},{6,7},{7,8},{8,9},{9,10},{10,1... | collective-permute-start | bytes 36872 | tf_op jit(solution)/shard_map/ppermute | solution.py:360
  24.6 4.4 %collective-permute-start.3 = (f32[24,128]{1,0:T(8,128)S(1)}, f32[24,128]{1,0:T(8,128)S(1)}, u32[]{:S(2)}, u32[]{:S(2)}) collective-permute-start(f32[24,128]{1,0:T(8,128)S(1)} %get-tuple-element.27), channel_id=1, source_target_pairs={{0,16},{16,0},{32,48},{48,32},{64,80},{80,64},{96,112},{112,96},{1... | collective-permute-start | bytes 36872 | tf_op jit(solution)/shard_map/ppermute | solution.py:365
  26.5 12.6 %copy-start = (bf16[8,1,1,8,48,48]{5,4,3,2,1,0:T(8,128)(2,1)S(1)}, bf16[8,1,1,8,48,48]{5,4,3,2,1,0:T(8,128)(2,1)}, u32[]{:S(2)}) copy-start(bf16[8,1,1,8,48,48]{5,4,3,2,1,0:T(8,128)(2,1)} %param.13) | copy-start | bytes 884740
  29.8 7.7 %collective-permute-start.7 = (f32[8,48]{1,0:T(8,128)S(1)}, f32[8,48]{1,0:T(8,128)S(1)}, u32[]{:S(2)}, u32[]{:S(2)}) collective-permute-start(f32[8,48]{1,0:T(8,128)S(1)} %get-tuple-element.29.approx_ref), channel_id=1, source_target_pairs={{0,1008},{16,32},{32,16},{48,64},{64,48},{80,96},{96,80},{112,128}... | collective-permute-start | bytes 4616 | tf_op jit(solution)/shard_map/ppermute | solution.py:365
  31.7 5.8 %collective-permute-start.6 = (f32[8,48]{1,0:T(8,128)S(1)}, f32[8,48]{1,0:T(8,128)S(1)}, u32[]{:S(2)}, u32[]{:S(2)}) collective-permute-start(f32[8,48]{1,0:T(8,128)S(1)} %get-tuple-element.29.approx_ref), channel_id=1, source_target_pairs={{0,15},{1,0},{2,1},{3,2},{4,3},{5,4},{6,5},{7,6},{8,7},{9,8},{10,9... | collective-permute-start | bytes 4616 | tf_op jit(solution)/shard_map/ppermute | solution.py:360
  31.8 5.8 %collective-permute-start.5 = (f32[8,48]{1,0:T(8,128)S(1)}, f32[8,48]{1,0:T(8,128)S(1)}, u32[]{:S(2)}, u32[]{:S(2)}) collective-permute-start(f32[8,48]{1,0:T(8,128)S(1)} %get-tuple-element.29.approx_ref), channel_id=1, source_target_pairs={{0,1},{1,2},{2,3},{3,4},{4,5},{5,6},{6,7},{7,8},{8,9},{9,10},{10,1... | collective-permute-start | bytes 4616 | tf_op jit(solution)/shard_map/ppermute | solution.py:360
  34.7 4.3 %collective-permute-start.4 = (f32[8,48]{1,0:T(8,128)S(1)}, f32[8,48]{1,0:T(8,128)S(1)}, u32[]{:S(2)}, u32[]{:S(2)}) collective-permute-start(f32[8,48]{1,0:T(8,128)S(1)} %get-tuple-element.29.approx_ref), channel_id=1, source_target_pairs={{0,16},{16,0},{32,48},{48,32},{64,80},{80,64},{96,112},{112,96},{1... | collective-permute-start | bytes 4616 | tf_op jit(solution)/shard_map/ppermute | solution.py:365
  39.6 11.6 %collective-permute-start.11 = (f32[8,48]{1,0:T(8,128)S(1)}, f32[8,48]{1,0:T(8,128)S(1)}, u32[]{:S(2)}, u32[]{:S(2)}) collective-permute-start(f32[8,48]{1,0:T(8,128)S(1)} %shard_map.89.approx_ref), channel_id=1, source_target_pairs={{0,1008},{16,32},{32,16},{48,64},{64,48},{80,96},{96,80},{112,128}... | collective-permute-start | bytes 4616 | tf_op jit(solution)/shard_map/ppermute | solution.py:365
  46.3 4.9 %collective-permute-start.10 = (f32[8,48]{1,0:T(8,128)S(1)}, f32[8,48]{1,0:T(8,128)S(1)}, u32[]{:S(2)}, u32[]{:S(2)}) collective-permute-start(f32[8,48]{1,0:T(8,128)S(1)} %shard_map.89.approx_ref), channel_id=1, source_target_pairs={{0,15},{1,0},{2,1},{3,2},{4,3},{5,4},{6,5},{7,6},{8,7},{9,8},{10,9... | collective-permute-start | bytes 4616 | tf_op jit(solution)/shard_map/ppermute | solution.py:360
  46.3 4.9 %collective-permute-start.9 = (f32[8,48]{1,0:T(8,128)S(1)}, f32[8,48]{1,0:T(8,128)S(1)}, u32[]{:S(2)}, u32[]{:S(2)}) collective-permute-start(f32[8,48]{1,0:T(8,128)S(1)} %shard_map.89.approx_ref), channel_id=1, source_target_pairs={{0,1},{1,2},{2,3},{3,4},{4,5},{5,6},{6,7},{7,8},{8,9},{9,10},{10,1... | collective-permute-start | bytes 4616 | tf_op jit(solution)/shard_map/ppermute | solution.py:360
  49.3 4.3 %collective-permute-start.8 = (f32[8,48]{1,0:T(8,128)S(1)}, f32[8,48]{1,0:T(8,128)S(1)}, u32[]{:S(2)}, u32[]{:S(2)}) collective-permute-start(f32[8,48]{1,0:T(8,128)S(1)} %shard_map.89.approx_ref), channel_id=1, source_target_pairs={{0,16},{16,0},{32,48},{48,32},{64,80},{80,64},{96,112},{112,96},{1... | collective-permute-start | bytes 4616 | tf_op jit(solution)/shard_map/ppermute | solution.py:365
  55.0 7.8 %collective-permute-start.12 = (f32[24,128]{1,0:T(8,128)S(1)}, f32[24,128]{1,0:T(8,128)S(1)}, u32[]{:S(2)}, u32[]{:S(2)}) collective-permute-start(f32[24,128]{1,0:T(8,128)S(1)} %get-tuple-element.36), channel_id=1, source_target_pairs={{0,1008},{16,32},{32,16},{48,64},{64,48},{80,96},{96,80},{112,128}... | collective-permute-start | bytes 36872 | tf_op jit(solution)/shard_map/ppermute | solution.py:365
  56.9 5.8 %collective-permute-start.13 = (f32[24,128]{1,0:T(8,128)S(1)}, f32[24,128]{1,0:T(8,128)S(1)}, u32[]{:S(2)}, u32[]{:S(2)}) collective-permute-start(f32[24,128]{1,0:T(8,128)S(1)} %get-tuple-element.37), channel_id=1, source_target_pairs={{0,15},{1,0},{2,1},{3,2},{4,3},{5,4},{6,5},{7,6},{8,7},{9,8},{10,9... | collective-permute-start | bytes 36872 | tf_op jit(solution)/shard_map/ppermute | solution.py:360
  56.9 5.8 %collective-permute-start.14 = (f32[24,128]{1,0:T(8,128)S(1)}, f32[24,128]{1,0:T(8,128)S(1)}, u32[]{:S(2)}, u32[]{:S(2)}) collective-permute-start(f32[24,128]{1,0:T(8,128)S(1)} %get-tuple-element.38), channel_id=1, source_target_pairs={{0,1},{1,2},{2,3},{3,4},{4,5},{5,6},{6,7},{7,8},{8,9},{9,10},{10,1... | collective-permute-start | bytes 36872 | tf_op jit(solution)/shard_map/ppermute | solution.py:360
  59.9 4.4 %collective-permute-start.15 = (f32[24,128]{1,0:T(8,128)S(1)}, f32[24,128]{1,0:T(8,128)S(1)}, u32[]{:S(2)}, u32[]{:S(2)}) collective-permute-start(f32[24,128]{1,0:T(8,128)S(1)} %get-tuple-element.39), channel_id=1, source_target_pairs={{0,16},{16,0},{32,48},{48,32},{64,80},{80,64},{96,112},{112,96},{1... | collective-permute-start | bytes 36872 | tf_op jit(solution)/shard_map/ppermute | solution.py:365
